TPU v7x, 256 devices: a whole 4x4x8 slice. The times are simulated.
256 devices in a mesh: tm: 8 (over x, core), space: 32 (over z, y).
Axes of the slice: x: 4, y: 4, z: 8, core: 2. Of those that a mesh axis runs over, the one named last changes fastest.
Arguments:
- fraction_levels: int32 [8, 128, 16, 1024], P('tm', 'space'), may hold values from 0 to 1024
- start_velocity: float32 [8, 3, 128, 16, 1024], P('tm', None, 'space'), may hold values from -1.8 to 1.8
- electrode_plan: int32 [16, 4, 32], P('tm'), may hold values 0 or 1
Outputs:
- end_fraction: float32 [8, 128, 16, 1024], P('tm', 'space')
- end_velocity: float32 [8, 3, 128, 16, 1024], P('tm', None, 'space')
All inputs are finite; a program needn't handle non-finite values. No bound on the sum of `electrode_plan` on one device may be relied on, other than what follows from the above.
Results may differ from a plain program's by a relative error of at most 0.00002.
Values sent between devices are 32-bit elements; how exact they have to be, the bound alone decides.
A program may use at most 128 MiB of HBM per device.

v0:
```python
import jax
import jax.numpy as jnp
from jax import lax
from jax.sharding import PartitionSpec as P

TILE = 32
FINE = 2
SWEEPS = 4
COARSE_STEPS = 2


liquid_density = 1.0
vapour_density = 0.1
viscosity = 0.1
time_step = 0.25
pull_strength = 1.5
wall_decay = 4.0
fraction_spread = 0.05
velocity_spread = 0.15
level_count = 1024.0


def padded_2(block, sides, width):
    for axis, dim in sides:
        count = lax.axis_size(axis)
        forward = [(i, i + 1) for i in range(count - 1)]
        backward = [(target, source) for source, target in forward]
        low = lax.ppermute(
            lax.slice_in_dim(block, block.shape[dim] - width, None, axis=dim), axis, forward
        )
        high = lax.ppermute(lax.slice_in_dim(block, 0, width, axis=dim), axis, backward)
        block = jnp.concatenate([low, block, high], axis=dim)
    return block


def shifted(value, axis, by):
    length = lax.axis_size(axis)
    pairs = [(i, i + by) for i in range(length) if 0 <= i + by < length]
    return lax.ppermute(value, axis, pairs)


def side_pad(array):
    widths = [(0, 0)] * (array.ndim - 2) + [(1, 1), (1, 1)]
    return jnp.pad(array, widths)


def neighbours(padded):
    return (
        padded[..., 2:, 1:-1, 1:-1]
        + padded[..., :-2, 1:-1, 1:-1]
        + padded[..., 1:-1, 2:, 1:-1]
        + padded[..., 1:-1, :-2, 1:-1]
        + padded[..., 1:-1, 1:-1, 2:]
        + padded[..., 1:-1, 1:-1, :-2]
    )


def centred(padded):
    return jnp.stack(
        [
            0.5 * (padded[2:, 1:-1, 1:-1] - padded[:-2, 1:-1, 1:-1]),
            0.5 * (padded[1:-1, 2:, 1:-1] - padded[1:-1, :-2, 1:-1]),
            0.5 * (padded[1:-1, 1:-1, 2:] - padded[1:-1, 1:-1, :-2]),
        ]
    )


def divergence(padded):
    return 0.5 * (
        padded[0, 2:, 1:-1, 1:-1]
        - padded[0, :-2, 1:-1, 1:-1]
        + padded[1, 1:-1, 2:, 1:-1]
        - padded[1, 1:-1, :-2, 1:-1]
        + padded[2, 1:-1, 1:-1, 2:]
        - padded[2, 1:-1, 1:-1, :-2]
    )


def density(fraction):
    return vapour_density + (liquid_density - vapour_density) * jnp.clip(fraction, 0.0, 1.0)


def face_flux(lower, upper, speed_lower, speed_upper):
    speed = 0.5 * (speed_lower + speed_upper)
    return jnp.maximum(speed, 0.0) * lower + jnp.minimum(speed, 0.0) * upper


def advect(cpad, upad):
    flux_x = face_flux(
        cpad[:-1, 1:-1, 1:-1],
        cpad[1:, 1:-1, 1:-1],
        upad[0, :-1, 1:-1, 1:-1],
        upad[0, 1:, 1:-1, 1:-1],
    )
    flux_z = face_flux(
        cpad[1:-1, :-1, 1:-1],
        cpad[1:-1, 1:, 1:-1],
        upad[1, 1:-1, :-1, 1:-1],
        upad[1, 1:-1, 1:, 1:-1],
    )
    flux_y = face_flux(
        cpad[1:-1, 1:-1, :-1],
        cpad[1:-1, 1:-1, 1:],
        upad[2, 1:-1, 1:-1, :-1],
        upad[2, 1:-1, 1:-1, 1:],
    )
    net = (
        flux_x[1:]
        - flux_x[:-1]
        + flux_z[:, 1:]
        - flux_z[:, :-1]
        + flux_y[:, :, 1:]
        - flux_y[:, :, :-1]
    )
    return cpad[1:-1, 1:-1, 1:-1] - time_step * net


def momentum(cpad, upad, electrode, wall):
    inner = upad[:, 1:-1, 1:-1, 1:-1]
    laplace = neighbours(upad) - 6.0 * inner
    pull = (
        pull_strength
        * electrode[:, None, :]
        * wall[None, :, None]
        / density(cpad[1:-1, 1:-1, 1:-1])
    )
    return inner + time_step * (viscosity * laplace + pull * centred(cpad))


def coefficients(fpad):
    rho = density(fpad)
    face_x = 2.0 / (rho[:-1, 1:-1, 1:-1] + rho[1:, 1:-1, 1:-1])
    face_z = 2.0 / (rho[1:-1, :-1, 1:-1] + rho[1:-1, 1:, 1:-1])
    face_y = 2.0 / (rho[1:-1, 1:-1, :-1] + rho[1:-1, 1:-1, 1:])
    total = (
        face_x[:-1]
        + face_x[1:]
        + face_z[:, :-1]
        + face_z[:, 1:]
        + face_y[:, :, :-1]
        + face_y[:, :, 1:]
    )
    return (face_x, face_z, face_y, total)


def jacobi(ppad, faces, total, source):
    face_x, face_z, face_y = faces
    summed = (
        face_x[:-1] * ppad[:-2, 1:-1, 1:-1]
        + face_x[1:] * ppad[2:, 1:-1, 1:-1]
        + face_z[:, :-1] * ppad[1:-1, :-2, 1:-1]
        + face_z[:, 1:] * ppad[1:-1, 2:, 1:-1]
        + face_y[:, :, :-1] * ppad[1:-1, 1:-1, :-2]
        + face_y[:, :, 1:] * ppad[1:-1, 1:-1, 2:]
    )
    return (summed - source) / total


def relax_round(pressure, faces, total, source, inside, depth):
    current = padded_2(pressure, (("space", 0),), depth)
    length = current.shape[0] - 2
    sliced = (faces[0], faces[1], faces[2])
    current = jacobi(side_pad(current), sliced, total, source)
    current = current * inside[0:length, None, None]
    return current


def fine_step(fraction, velocity, electrode, wall, depth, inside):
    stacked = jnp.concatenate([fraction[None], velocity])
    padded = side_pad(padded_2(stacked, (("space", 1),), 1))
    new_fraction = advect(padded[0], padded[1:])
    provisional = momentum(padded[0], padded[1:], electrode, wall)
    second_stack = jnp.concatenate([new_fraction[None], provisional])
    second = side_pad(padded_2(second_stack, (("space", 1),), depth))
    face_x, face_z, face_y, total = coefficients(second[0])
    source = divergence(second[1:]) / time_step

    def round_once(index, current):
        return relax_round(current, (face_x, face_z, face_y), total, source, inside, depth)

    pressure = lax.fori_loop(0, SWEEPS // depth, round_once, jnp.zeros_like(new_fraction))
    ppad = side_pad(padded_2(pressure, (("space", 0),), 1))
    return (new_fraction, provisional - time_step * centred(ppad) / density(new_fraction))


def restrict(field):
    parts, rows, layers, columns = field.shape
    blocks = field.reshape(parts, rows // 4, 4, layers // 4, 4, columns // 4, 4)
    return jnp.mean(blocks, axis=(2, 4, 6))


def prolong(coarse):
    parts, rows, layers, columns = coarse.shape
    wide = jnp.broadcast_to(
        coarse[:, :, None, :, None, :, None], (parts, rows, 4, layers, 4, columns, 4)
    )
    return wide.reshape(parts, rows * 4, layers * 4, columns * 4)


def propagate(coarse):
    spreads = jnp.array(
        [fraction_spread, velocity_spread, velocity_spread, velocity_spread], dtype=jnp.float32
    )
    spreads = spreads[:, None, None, None]
    for step in range(COARSE_STEPS):
        extended = padded_2(coarse, (("space", 1),), 1)
        padded = side_pad(extended)
        coarse = coarse + spreads * (neighbours(padded) - 6.0 * coarse)
    return coarse


def electrode_field(plan_row, first_row, rows):
    tiles = (first_row + jnp.arange(rows, dtype=jnp.int32)) // TILE
    picker = (tiles[:, None] == jnp.arange(plan_row.shape[0], dtype=jnp.int32)[None, :]).astype(
        jnp.float32
    )
    chosen = jnp.sum(picker[:, :, None] * plan_row.astype(jnp.float32)[None], axis=1)
    wide = jnp.broadcast_to(chosen[:, :, None], chosen.shape + (TILE,))
    return wide.reshape(rows, chosen.shape[1] * TILE)


def shards(fraction_levels, start_velocity, electrode_plan):
    fraction = fraction_levels[0].astype(jnp.float32) / level_count
    velocity = start_velocity[0]
    rows = fraction.shape[0]
    first_row = lax.axis_index("space") * rows
    wall = jnp.exp(-jnp.arange(fraction.shape[1], dtype=jnp.float32) / wall_decay)
    depth = 1
    grid_rows = rows * lax.axis_size("space")
    places = first_row - (depth - 1) + jnp.arange(rows + 2 * depth - 2, dtype=jnp.int32)
    inside = ((places >= 0) & (places < grid_rows)).astype(jnp.float32)
    start = jnp.concatenate([fraction[None], velocity])
    for step in range(FINE):
        electrode = electrode_field(electrode_plan[step], first_row, rows)
        fraction, velocity = fine_step(fraction, velocity, electrode, wall, depth, inside)
    fine_end = jnp.concatenate([fraction[None], velocity])
    coarse_start = restrict(start)
    coarse_end = restrict(fine_end)
    later = (lax.axis_index("tm") > 0).astype(jnp.float32)
    previous = propagate(coarse_start) * later
    drive = coarse_end - previous
    slices_count = lax.axis_size("tm")

    def advance(index, carry):
        return shifted(propagate(carry) + drive, "tm", 1)

    carry = lax.fori_loop(0, slices_count - 1, advance, jnp.zeros_like(drive))
    correction = propagate(carry) - previous
    corrected = fine_end + prolong(correction)
    return (corrected[0][None], corrected[1:][None])


def solution(mesh):
    return jax.shard_map(
        shards,
        mesh=mesh,
        in_specs=(
            P("tm", "space", None, None),
            P("tm", None, "space", None, None),
            P("tm", None, None),
        ),
        out_specs=(P("tm", "space", None, None), P("tm", None, "space", None, None)),
        check_vma=False,
    )
```

profile of v0, /device:TPU:126, one launch (start us, length us, event | category | flops | bytes accessed | tf_op | source)
XLA Modules:
  0.0 546.3 jit_solution(7927878317986623687)
XLA Ops:
  2.9 2.7 collective-permute-start.10
  5.5 6.5 %collective-permute-start.9 = (f32[4,1,16,1024]{3,2,1,0:T(8,128)S(1)}, f32[4,1,16,1024]{3,2,1,0:T(8,128)S(1)}, u32[]{:S(2)}, u32[]{:S(2)}) collective-permute-start(f32[4,1,16,1024]{3,2,1,0:T(8,128)S(1)} %get-tuple-element.388), channel_id=1, source_target_pairs={{0,1},{1,2},{2,3},{3,4},{4,5},{5,6},{6,7},{7,8},{8,9},{9,10},{10,1... | collective-permute-start | bytes 786440 | tf_op jit(solution)/shard_map/ppermute | solution.py:28
  13.1 3.0 collective-permute-done.10
  21.3 7.7 %collective-permute-start.11 = (f32[4,1,16,1024]{3,2,1,0:T(8,128)S(1)}, f32[4,1,16,1024]{3,2,1,0:T(8,128)S(1)}, u32[]{:S(2)}, u32[]{:S(2)}) collective-permute-start(f32[4,1,16,1024]{3,2,1,0:T(8,128)S(1)} %get-tuple-element.386), channel_id=1, source_target_pairs={{0,1},{1,2},{2,3},{3,4},{4,5},{5,6},{6,7},{7,8},{8,9},{9,10},{10,1... | collective-permute-start | bytes 786440 | tf_op jit(solution)/shard_map/ppermute | solution.py:28
  30.9 2.4 collective-permute-done.11
  33.3 7.4 %collective-permute-done.12 = f32[4,1,16,1024]{3,2,1,0:T(8,128)S(1)} collective-permute-done((f32[4,1,16,1024]{3,2,1,0:T(8,128)S(1)}, f32[4,1,16,1024]{3,2,1,0:T(8,128)S(1)}, u32[]{:S(2)}, u32[]{:S(2)}) %collective-permute-start.12) | collective-permute-done | bytes 262176 | tf_op jit(solution)/shard_map/ppermute | solution.py:31
  44.2 52.1 %while.40 = (s32[]{:T(128)}, f32[4,16,1024]{2,1,0:T(8,128)S(1)}, f32[5,16,1024]{2,1,0:T(8,128)S(1)}, f32[4,17,1024]{2,1,0:T(8,128)S(1)}, f32[4,16,1025]{2,1,0:T(...) while((s32[]{:T(128)}, f32[4,16,1024]{2,1,0:T(8,128)S(1)}, ...), condition=%wide.region_2.3_spmd.clone, body=%wide.region_1.2_spmd.clone.sunk | while | flops 2776255 | bytes 5948483 | solution.py:181
  46.2 7.2 %collective-permute-start.6 = (f32[1,16,1024]{2,1,0:T(8,128)S(1)}, f32[1,16,1024]{2,1,0:T(8,128)S(1)}, u32[]{:S(2)}, u32[]{:S(2)}) collective-permute-start(f32[1,16,1024]{2,1,0:T(8,128)S(1)} %get-tuple-element.528), channel_id=1, source_target_pairs={{0,1},{1,2},{2,3},{3,4},{4,5},{5,6},{6,7},{7,8},{8,9},{9,10},{10,1... | collective-permute-start | bytes 196616 | tf_op jit(solution)/shard_map/while/body/eval_jaxpr/ppermute | solution.py:28
  58.9 7.6 %collective-permute-start.6 = (f32[1,16,1024]{2,1,0:T(8,128)S(1)}, f32[1,16,1024]{2,1,0:T(8,128)S(1)}, u32[]{:S(2)}, u32[]{:S(2)}) collective-permute-start(f32[1,16,1024]{2,1,0:T(8,128)S(1)} %get-tuple-element.528), channel_id=1, source_target_pairs={{0,1},{1,2},{2,3},{3,4},{4,5},{5,6},{6,7},{7,8},{8,9},{9,10},{10,1... | collective-permute-start | bytes 196616 | tf_op jit(solution)/shard_map/while/body/eval_jaxpr/ppermute | solution.py:28
  70.1 1.9 collective-permute-start.5
  72.1 7.6 %collective-permute-start.6 = (f32[1,16,1024]{2,1,0:T(8,128)S(1)}, f32[1,16,1024]{2,1,0:T(8,128)S(1)}, u32[]{:S(2)}, u32[]{:S(2)}) collective-permute-start(f32[1,16,1024]{2,1,0:T(8,128)S(1)} %get-tuple-element.528), channel_id=1, source_target_pairs={{0,1},{1,2},{2,3},{3,4},{4,5},{5,6},{6,7},{7,8},{8,9},{9,10},{10,1... | collective-permute-start | bytes 196616 | tf_op jit(solution)/shard_map/while/body/eval_jaxpr/ppermute | solution.py:28
  83.3 1.9 collective-permute-start.5
  85.2 7.6 %collective-permute-start.6 = (f32[1,16,1024]{2,1,0:T(8,128)S(1)}, f32[1,16,1024]{2,1,0:T(8,128)S(1)}, u32[]{:S(2)}, u32[]{:S(2)}) collective-permute-start(f32[1,16,1024]{2,1,0:T(8,128)S(1)} %get-tuple-element.528), channel_id=1, source_target_pairs={{0,1},{1,2},{2,3},{3,4},{4,5},{5,6},{6,7},{7,8},{8,9},{9,10},{10,1... | collective-permute-start | bytes 196616 | tf_op jit(solution)/shard_map/while/body/eval_jaxpr/ppermute | solution.py:28
  96.3 1.9 collective-permute-start.13
  98.3 7.6 %collective-permute-start.14 = (f32[1,16,1024]{2,1,0:T(8,128)S(1)}, f32[1,16,1024]{2,1,0:T(8,128)S(1)}, u32[]{:S(2)}, u32[]{:S(2)}) collective-permute-start(f32[1,16,1024]{2,1,0:T(8,128)S(1)} %get-tuple-element.408), channel_id=1, source_target_pairs={{0,1},{1,2},{2,3},{3,4},{4,5},{5,6},{6,7},{7,8},{8,9},{9,10},{10,1... | collective-permute-start | bytes 196616 | tf_op jit(solution)/shard_map/ppermute | solution.py:28
  105.9 10.8 %concatenate.174 = f32[1,1,4,4,4,256,4]{6,5,4,3,2,1,0:T(8,128)} reshape(f32[1,4,16,1024]{3,2,1,0:T(8,128)} %copy-done.1) | data formatting | bytes 524288 | tf_op jit(solution)/shard_map/concatenate | solution.py:169
  116.7 27.4 %concatenate.175 = f32[3,1,4,4,4,256,4]{6,5,4,3,2,0,1:T(8,128)} reshape(f32[1,3,4,16,1024]{4,3,2,1,0:T(8,128)S(1)} %copy-done) | data formatting | bytes 1572864 | tf_op jit(solution)/shard_map/concatenate | solution.py:169
  144.1 5.9 %copy.42 = f32[1,1,4,4,4,256,4]{5,6,4,3,2,1,0:T(4,128)} copy(f32[1,1,4,4,4,256,4]{6,5,4,3,2,1,0:T(8,128)} %concatenate.174) | data formatting | bytes 524288 | tf_op jit(solution)/shard_map/concatenate | solution.py:169
  149.9 14.7 %copy.43 = f32[3,1,4,4,4,256,4]{5,6,4,3,2,1,0:T(4,128)S(1)} copy(f32[3,1,4,4,4,256,4]{6,5,4,3,2,0,1:T(8,128)} %concatenate.175) | data formatting | bytes 1572864 | tf_op jit(solution)/shard_map/concatenate | solution.py:169
  165.9 3.9 collective-permute-start.15
  173.9 7.4 %collective-permute-start.22 = (f32[4,1,4,256]{3,2,0,1:T(4,128)S(1)}, f32[4,1,4,256]{3,2,0,1:T(4,128)S(1)}, u32[]{:S(2)}, u32[]{:S(2)}) collective-permute-start(f32[4,1,4,256]{3,2,0,1:T(4,128)S(1)} %multiply_bitcast_fusion), channel_id=1, source_target_pairs={{0,1},{1,2},{2,3},{3,4},{4,5},{5,6},{6,7},{7,8},{8,9},{9,10},{10,1... | collective-permute-start | bytes 49160 | tf_op jit(solution)/shard_map/ppermute | solution.py:28
  184.9 3.9 collective-permute-start.17
  188.8 1.9 collective-permute-start.18
  192.9 7.2 %collective-permute-start.24 = (f32[4,1,4,256]{3,2,0,1:T(4,128)S(1)}, f32[4,1,4,256]{3,2,0,1:T(4,128)S(1)}, u32[]{:S(2)}, u32[]{:S(2)}) collective-permute-start(f32[4,1,4,256]{3,2,0,1:T(4,128)S(1)} %fusion.164), channel_id=1, source_target_pairs={{0,1},{1,2},{2,3},{3,4},{4,5},{5,6},{6,7},{7,8},{8,9},{9,10},{10,1... | collective-permute-start | bytes 49160 | tf_op jit(solution)/shard_map/ppermute | solution.py:28
  202.6 48.3 %while.41 = (s32[]{:T(128)}, f32[4,16,1024]{2,1,0:T(8,128)S(1)}, f32[5,16,1024]{2,1,0:T(8,128)S(1)}, f32[4,17,1024]{2,1,0:T(8,128)S(1)}, f32[4,16,1025]{2,1,0:T(...) while((s32[]{:T(128)}, f32[4,16,1024]{2,1,0:T(8,128)S(1)}, ...), condition=%wide.region_5.6_spmd.clone, body=%wide.region_4.5_spmd.clone.sunk | while | flops 2776255 | bytes 5948483 | solution.py:181
  204.6 7.3 %collective-permute-start.8 = (f32[1,16,1024]{2,1,0:T(8,128)S(1)}, f32[1,16,1024]{2,1,0:T(8,128)S(1)}, u32[]{:S(2)}, u32[]{:S(2)}) collective-permute-start(f32[1,16,1024]{2,1,0:T(8,128)S(1)} %get-tuple-element.538), channel_id=1, source_target_pairs={{0,1},{1,2},{2,3},{3,4},{4,5},{5,6},{6,7},{7,8},{8,9},{9,10},{10,1... | collective-permute-start | bytes 196616 | tf_op jit(solution)/shard_map/while/body/eval_jaxpr/ppermute | solution.py:28
  214.5 1.9 collective-permute-start.7
  216.4 7.7 %collective-permute-start.8 = (f32[1,16,1024]{2,1,0:T(8,128)S(1)}, f32[1,16,1024]{2,1,0:T(8,128)S(1)}, u32[]{:S(2)}, u32[]{:S(2)}) collective-permute-start(f32[1,16,1024]{2,1,0:T(8,128)S(1)} %get-tuple-element.538), channel_id=1, source_target_pairs={{0,1},{1,2},{2,3},{3,4},{4,5},{5,6},{6,7},{7,8},{8,9},{9,10},{10,1... | collective-permute-start | bytes 196616 | tf_op jit(solution)/shard_map/while/body/eval_jaxpr/ppermute | solution.py:28
  226.7 1.9 collective-permute-start.7
  228.7 7.6 %collective-permute-start.8 = (f32[1,16,1024]{2,1,0:T(8,128)S(1)}, f32[1,16,1024]{2,1,0:T(8,128)S(1)}, u32[]{:S(2)}, u32[]{:S(2)}) collective-permute-start(f32[1,16,1024]{2,1,0:T(8,128)S(1)} %get-tuple-element.538), channel_id=1, source_target_pairs={{0,1},{1,2},{2,3},{3,4},{4,5},{5,6},{6,7},{7,8},{8,9},{9,10},{10,1... | collective-permute-start | bytes 196616 | tf_op jit(solution)/shard_map/while/body/eval_jaxpr/ppermute | solution.py:28
  240.8 7.6 %collective-permute-start.8 = (f32[1,16,1024]{2,1,0:T(8,128)S(1)}, f32[1,16,1024]{2,1,0:T(8,128)S(1)}, u32[]{:S(2)}, u32[]{:S(2)}) collective-permute-start(f32[1,16,1024]{2,1,0:T(8,128)S(1)} %get-tuple-element.538), channel_id=1, source_target_pairs={{0,1},{1,2},{2,3},{3,4},{4,5},{5,6},{6,7},{7,8},{8,9},{9,10},{10,1... | collective-permute-start | bytes 196616 | tf_op jit(solution)/shard_map/while/body/eval_jaxpr/ppermute | solution.py:28
  252.9 7.6 %collective-permute-start.20 = (f32[1,16,1024]{2,1,0:T(8,128)S(1)}, f32[1,16,1024]{2,1,0:T(8,128)S(1)}, u32[]{:S(2)}, u32[]{:S(2)}) collective-permute-start(f32[1,16,1024]{2,1,0:T(8,128)S(1)} %get-tuple-element.406), channel_id=1, source_target_pairs={{0,1},{1,2},{2,3},{3,4},{4,5},{5,6},{6,7},{7,8},{8,9},{9,10},{10,1... | collective-permute-start | bytes 196616 | tf_op jit(solution)/shard_map/ppermute | solution.py:28
  260.6 10.1 %concatenate.171 = f32[1,1,4,4,4,256,4]{6,5,4,3,2,1,0:T(8,128)} reshape(f32[4,16,1024]{2,1,0:T(8,128)S(1)} %get-tuple-element.397) | data formatting | bytes 524288 | tf_op jit(solution)/shard_map/concatenate | solution.py:236
  270.7 5.2 copy.40
  277.0 27.4 %concatenate.172 = f32[3,1,4,4,4,256,4]{6,5,4,3,2,0,1:T(8,128)} reshape(f32[3,4,16,1024]{3,2,1,0:T(8,128)S(1)} %fusion.67) | data formatting | bytes 1572864 | tf_op jit(solution)/shard_map/concatenate | solution.py:236
  304.4 14.7 %copy.41 = f32[3,1,4,4,4,256,4]{5,6,4,3,2,1,0:T(4,128)S(1)} copy(f32[3,1,4,4,4,256,4]{6,5,4,3,2,0,1:T(8,128)} %concatenate.172) | data formatting | bytes 1572864 | tf_op jit(solution)/shard_map/concatenate | solution.py:236
  319.6 190.5 %while.39 = (s32[]{:T(128)}, f32[4,1,4,256]{3,2,1,0:T(4,128)S(1)}, f32[4,1,4,256]{3,2,1,0:T(4,128)S(1)}, s32[]{:T(128)}, f32[4]{0:T(128)S(1)}) while((s32[]{:T(128)}, f32[4,1,4,256]{3,2,1,0:T(4,128)S(1)}, f32[4,1,4,256]{3,2,1,0:T(4,128)S(1)}, s32[]{:T(128)}, f32[4]{0:T(128)S(1)}) %tuple.123), condition=%wide.region_9.10_spmd.clone, body=%wide.region_8.9_spmd.sunk.clone.sunk | while | flops 635106 | bytes 853413 | solution.py:247
  321.5 7.2 %collective-permute-start.1 = (f32[4,1,4,256]{3,2,1,0:T(4,128)S(1)}, f32[4,1,4,256]{3,2,1,0:T(4,128)S(1)}, u32[]{:S(2)}, u32[]{:S(2)}) collective-permute-start(f32[4,1,4,256]{3,2,1,0:T(4,128)S(1)} %get-tuple-element.605), channel_id=1, source_target_pairs={{0,1},{1,2},{2,3},{3,4},{4,5},{5,6},{6,7},{7,8},{8,9},{9,10},{10,1... | collective-permute-start | bytes 49160 | tf_op jit(solution)/shard_map/while/body/eval_jaxpr/ppermute | solution.py:28
  330.4 1.9 collective-permute-start.2
  332.3 7.5 %collective-permute-start.3 = (f32[4,1,4,256]{3,2,1,0:T(4,128)S(1)}, f32[4,1,4,256]{3,2,1,0:T(4,128)S(1)}, u32[]{:S(2)}, u32[]{:S(2)}) collective-permute-start(f32[4,1,4,256]{3,2,1,0:T(4,128)S(1)} %fusion.179), channel_id=1, source_target_pairs={{0,1},{1,2},{2,3},{3,4},{4,5},{5,6},{6,7},{7,8},{8,9},{9,10},{10,1... | collective-permute-start | bytes 49160 | tf_op jit(solution)/shard_map/while/body/eval_jaxpr/ppermute | solution.py:28
  343.5 3.1 collective-permute-done.4
  348.5 7.5 %collective-permute-start.1 = (f32[4,1,4,256]{3,2,1,0:T(4,128)S(1)}, f32[4,1,4,256]{3,2,1,0:T(4,128)S(1)}, u32[]{:S(2)}, u32[]{:S(2)}) collective-permute-start(f32[4,1,4,256]{3,2,1,0:T(4,128)S(1)} %get-tuple-element.605), channel_id=1, source_target_pairs={{0,1},{1,2},{2,3},{3,4},{4,5},{5,6},{6,7},{7,8},{8,9},{9,10},{10,1... | collective-permute-start | bytes 49160 | tf_op jit(solution)/shard_map/while/body/eval_jaxpr/ppermute | solution.py:28
  357.7 1.9 collective-permute-start.2
  359.6 7.5 %collective-permute-start.3 = (f32[4,1,4,256]{3,2,1,0:T(4,128)S(1)}, f32[4,1,4,256]{3,2,1,0:T(4,128)S(1)}, u32[]{:S(2)}, u32[]{:S(2)}) collective-permute-start(f32[4,1,4,256]{3,2,1,0:T(4,128)S(1)} %fusion.179), channel_id=1, source_target_pairs={{0,1},{1,2},{2,3},{3,4},{4,5},{5,6},{6,7},{7,8},{8,9},{9,10},{10,1... | collective-permute-start | bytes 49160 | tf_op jit(solution)/shard_map/while/body/eval_jaxpr/ppermute | solution.py:28
  370.7 3.1 collective-permute-done.4
  375.8 7.5 %collective-permute-start.1 = (f32[4,1,4,256]{3,2,1,0:T(4,128)S(1)}, f32[4,1,4,256]{3,2,1,0:T(4,128)S(1)}, u32[]{:S(2)}, u32[]{:S(2)}) collective-permute-start(f32[4,1,4,256]{3,2,1,0:T(4,128)S(1)} %get-tuple-element.605), channel_id=1, source_target_pairs={{0,1},{1,2},{2,3},{3,4},{4,5},{5,6},{6,7},{7,8},{8,9},{9,10},{10,1... | collective-permute-start | bytes 49160 | tf_op jit(solution)/shard_map/while/body/eval_jaxpr/ppermute | solution.py:28
  386.9 7.5 %collective-permute-start.3 = (f32[4,1,4,256]{3,2,1,0:T(4,128)S(1)}, f32[4,1,4,256]{3,2,1,0:T(4,128)S(1)}, u32[]{:S(2)}, u32[]{:S(2)}) collective-permute-start(f32[4,1,4,256]{3,2,1,0:T(4,128)S(1)} %fusion.179), channel_id=1, source_target_pairs={{0,1},{1,2},{2,3},{3,4},{4,5},{5,6},{6,7},{7,8},{8,9},{9,10},{10,1... | collective-permute-start | bytes 49160 | tf_op jit(solution)/shard_map/while/body/eval_jaxpr/ppermute | solution.py:28
  398.0 3.1 collective-permute-done.4
  403.0 7.5 %collective-permute-start.1 = (f32[4,1,4,256]{3,2,1,0:T(4,128)S(1)}, f32[4,1,4,256]{3,2,1,0:T(4,128)S(1)}, u32[]{:S(2)}, u32[]{:S(2)}) collective-permute-start(f32[4,1,4,256]{3,2,1,0:T(4,128)S(1)} %get-tuple-element.605), channel_id=1, source_target_pairs={{0,1},{1,2},{2,3},{3,4},{4,5},{5,6},{6,7},{7,8},{8,9},{9,10},{10,1... | collective-permute-start | bytes 49160 | tf_op jit(solution)/shard_map/while/body/eval_jaxpr/ppermute | solution.py:28
  414.1 7.5 %collective-permute-start.3 = (f32[4,1,4,256]{3,2,1,0:T(4,128)S(1)}, f32[4,1,4,256]{3,2,1,0:T(4,128)S(1)}, u32[]{:S(2)}, u32[]{:S(2)}) collective-permute-start(f32[4,1,4,256]{3,2,1,0:T(4,128)S(1)} %fusion.179), channel_id=1, source_target_pairs={{0,1},{1,2},{2,3},{3,4},{4,5},{5,6},{6,7},{7,8},{8,9},{9,10},{10,1... | collective-permute-start | bytes 49160 | tf_op jit(solution)/shard_map/while/body/eval_jaxpr/ppermute | solution.py:28
  425.2 3.1 collective-permute-done.4
  430.3 7.5 %collective-permute-start.1 = (f32[4,1,4,256]{3,2,1,0:T(4,128)S(1)}, f32[4,1,4,256]{3,2,1,0:T(4,128)S(1)}, u32[]{:S(2)}, u32[]{:S(2)}) collective-permute-start(f32[4,1,4,256]{3,2,1,0:T(4,128)S(1)} %get-tuple-element.605), channel_id=1, source_target_pairs={{0,1},{1,2},{2,3},{3,4},{4,5},{5,6},{6,7},{7,8},{8,9},{9,10},{10,1... | collective-permute-start | bytes 49160 | tf_op jit(solution)/shard_map/while/body/eval_jaxpr/ppermute | solution.py:28
  441.4 7.5 %collective-permute-start.3 = (f32[4,1,4,256]{3,2,1,0:T(4,128)S(1)}, f32[4,1,4,256]{3,2,1,0:T(4,128)S(1)}, u32[]{:S(2)}, u32[]{:S(2)}) collective-permute-start(f32[4,1,4,256]{3,2,1,0:T(4,128)S(1)} %fusion.179), channel_id=1, source_target_pairs={{0,1},{1,2},{2,3},{3,4},{4,5},{5,6},{6,7},{7,8},{8,9},{9,10},{10,1... | collective-permute-start | bytes 49160 | tf_op jit(solution)/shard_map/while/body/eval_jaxpr/ppermute | solution.py:28
  452.5 3.1 collective-permute-done.4
  457.5 7.5 %collective-permute-start.1 = (f32[4,1,4,256]{3,2,1,0:T(4,128)S(1)}, f32[4,1,4,256]{3,2,1,0:T(4,128)S(1)}, u32[]{:S(2)}, u32[]{:S(2)}) collective-permute-start(f32[4,1,4,256]{3,2,1,0:T(4,128)S(1)} %get-tuple-element.605), channel_id=1, source_target_pairs={{0,1},{1,2},{2,3},{3,4},{4,5},{5,6},{6,7},{7,8},{8,9},{9,10},{10,1... | collective-permute-start | bytes 49160 | tf_op jit(solution)/shard_map/while/body/eval_jaxpr/ppermute | solution.py:28
  468.6 7.5 %collective-permute-start.3 = (f32[4,1,4,256]{3,2,1,0:T(4,128)S(1)}, f32[4,1,4,256]{3,2,1,0:T(4,128)S(1)}, u32[]{:S(2)}, u32[]{:S(2)}) collective-permute-start(f32[4,1,4,256]{3,2,1,0:T(4,128)S(1)} %fusion.179), channel_id=1, source_target_pairs={{0,1},{1,2},{2,3},{3,4},{4,5},{5,6},{6,7},{7,8},{8,9},{9,10},{10,1... | collective-permute-start | bytes 49160 | tf_op jit(solution)/shard_map/while/body/eval_jaxpr/ppermute | solution.py:28
  479.7 3.1 collective-permute-done.4
  484.8 7.5 %collective-permute-start.1 = (f32[4,1,4,256]{3,2,1,0:T(4,128)S(1)}, f32[4,1,4,256]{3,2,1,0:T(4,128)S(1)}, u32[]{:S(2)}, u32[]{:S(2)}) collective-permute-start(f32[4,1,4,256]{3,2,1,0:T(4,128)S(1)} %get-tuple-element.605), channel_id=1, source_target_pairs={{0,1},{1,2},{2,3},{3,4},{4,5},{5,6},{6,7},{7,8},{8,9},{9,10},{10,1... | collective-permute-start | bytes 49160 | tf_op jit(solution)/shard_map/while/body/eval_jaxpr/ppermute | solution.py:28
  495.9 7.5 %collective-permute-start.3 = (f32[4,1,4,256]{3,2,1,0:T(4,128)S(1)}, f32[4,1,4,256]{3,2,1,0:T(4,128)S(1)}, u32[]{:S(2)}, u32[]{:S(2)}) collective-permute-start(f32[4,1,4,256]{3,2,1,0:T(4,128)S(1)} %fusion.179), channel_id=1, source_target_pairs={{0,1},{1,2},{2,3},{3,4},{4,5},{5,6},{6,7},{7,8},{8,9},{9,10},{10,1... | collective-permute-start | bytes 49160 | tf_op jit(solution)/shard_map/while/body/eval_jaxpr/ppermute | solution.py:28
  507.0 3.1 collective-permute-done.4
  512.0 7.5 %collective-permute-start.26 = (f32[4,1,4,256]{3,2,1,0:T(4,128)S(1)}, f32[4,1,4,256]{3,2,1,0:T(4,128)S(1)}, u32[]{:S(2)}, u32[]{:S(2)}) collective-permute-start(f32[4,1,4,256]{3,2,1,0:T(4,128)S(1)} %get-tuple-element.259), channel_id=1, source_target_pairs={{0,1},{1,2},{2,3},{3,4},{4,5},{5,6},{6,7},{7,8},{8,9},{9,10},{10,1... | collective-permute-start | bytes 49160 | tf_op jit(solution)/shard_map/ppermute | solution.py:28
  523.1 7.5 %collective-permute-start.28 = (f32[4,1,4,256]{3,2,0,1:T(4,128)S(1)}, f32[4,1,4,256]{3,2,0,1:T(4,128)S(1)}, u32[]{:S(2)}, u32[]{:S(2)}) collective-permute-start(f32[4,1,4,256]{3,2,0,1:T(4,128)S(1)} %bitcast.124), channel_id=1, source_target_pairs={{0,1},{1,2},{2,3},{3,4},{4,5},{5,6},{6,7},{7,8},{8,9},{9,10},{10,1... | collective-permute-start | bytes 49160 | tf_op jit(solution)/shard_map/ppermute | solution.py:28
  532.3 3.8 broadcast_in_dim.27
  536.2 8.4 %broadcast_in_dim.28 = f32[4,16,1024]{2,1,0:T(8,128)S(1)} reshape(f32[4,4,4,256,4]{4,3,2,1,0:T(8,128)} %broadcast_in_dim.27) | data formatting | bytes 524288 | tf_op jit(solution)/shard_map/broadcast_in_dim | solution.py:194
  (245 shorter events, 130.5 us)
Async XLA Ops:
  2.9 13.3 %collective-permute-start.10 = (f32[4,1,16,1024]{3,2,1,0:T(8,128)S(1)}, f32[4,1,16,1024]{3,2,1,0:T(8,128)S(1)}, u32[]{:S(2)}, u32[]{:S(2)}) collective-permute-start(f32[4,1,16,1024]{3,2,1,0:T(8,128)S(1)} %get-tuple-element.389), channel_id=1, source_target_pairs={{1,0},{2,1},{3,2},{4,3},{5,4},{6,5},{7,6},{8,7},{9,8},{10,9},{11,1... | collective-permute-start | bytes 786440 | tf_op jit(solution)/shard_map/ppermute | solution.py:31
  5.5 11.8 %collective-permute-start.9 = (f32[4,1,16,1024]{3,2,1,0:T(8,128)S(1)}, f32[4,1,16,1024]{3,2,1,0:T(8,128)S(1)}, u32[]{:S(2)}, u32[]{:S(2)}) collective-permute-start(f32[4,1,16,1024]{3,2,1,0:T(8,128)S(1)} %get-tuple-element.388), channel_id=1, source_target_pairs={{0,1},{1,2},{2,3},{3,4},{4,5},{5,6},{6,7},{7,8},{8,9},{9,10},{10,1... | collective-permute-start | bytes 786440 | tf_op jit(solution)/shard_map/ppermute | solution.py:28
  21.3 12.1 %collective-permute-start.11 = (f32[4,1,16,1024]{3,2,1,0:T(8,128)S(1)}, f32[4,1,16,1024]{3,2,1,0:T(8,128)S(1)}, u32[]{:S(2)}, u32[]{:S(2)}) collective-permute-start(f32[4,1,16,1024]{3,2,1,0:T(8,128)S(1)} %get-tuple-element.386), channel_id=1, source_target_pairs={{0,1},{1,2},{2,3},{3,4},{4,5},{5,6},{6,7},{7,8},{8,9},{9,10},{10,1... | collective-permute-start | bytes 786440 | tf_op jit(solution)/shard_map/ppermute | solution.py:28
  29.0 11.8 %collective-permute-start.12 = (f32[4,1,16,1024]{3,2,1,0:T(8,128)S(1)}, f32[4,1,16,1024]{3,2,1,0:T(8,128)S(1)}, u32[]{:S(2)}, u32[]{:S(2)}) collective-permute-start(f32[4,1,16,1024]{3,2,1,0:T(8,128)S(1)} %get-tuple-element.387), channel_id=1, source_target_pairs={{1,0},{2,1},{3,2},{4,3},{5,4},{6,5},{7,6},{8,7},{9,8},{10,9},{11,1... | collective-permute-start | bytes 786440 | tf_op jit(solution)/shard_map/ppermute | solution.py:31
  44.2 9.5 %collective-permute-start.5 = (f32[1,16,1024]{2,1,0:T(8,128)S(1)}, f32[1,16,1024]{2,1,0:T(8,128)S(1)}, u32[]{:S(2)}, u32[]{:S(2)}) collective-permute-start(f32[1,16,1024]{2,1,0:T(8,128)S(1)} %get-tuple-element.527), channel_id=1, source_target_pairs={{1,0},{2,1},{3,2},{4,3},{5,4},{6,5},{7,6},{8,7},{9,8},{10,9},{11,1... | collective-permute-start | bytes 196616 | tf_op jit(solution)/shard_map/while/body/eval_jaxpr/ppermute | solution.py:31
  46.2 9.1 %collective-permute-start.6 = (f32[1,16,1024]{2,1,0:T(8,128)S(1)}, f32[1,16,1024]{2,1,0:T(8,128)S(1)}, u32[]{:S(2)}, u32[]{:S(2)}) collective-permute-start(f32[1,16,1024]{2,1,0:T(8,128)S(1)} %get-tuple-element.528), channel_id=1, source_target_pairs={{0,1},{1,2},{2,3},{3,4},{4,5},{5,6},{6,7},{7,8},{8,9},{9,10},{10,1... | collective-permute-start | bytes 196616 | tf_op jit(solution)/shard_map/while/body/eval_jaxpr/ppermute | solution.py:28
  57.0 9.8 %collective-permute-start.5 = (f32[1,16,1024]{2,1,0:T(8,128)S(1)}, f32[1,16,1024]{2,1,0:T(8,128)S(1)}, u32[]{:S(2)}, u32[]{:S(2)}) collective-permute-start(f32[1,16,1024]{2,1,0:T(8,128)S(1)} %get-tuple-element.527), channel_id=1, source_target_pairs={{1,0},{2,1},{3,2},{4,3},{5,4},{6,5},{7,6},{8,7},{9,8},{10,9},{11,1... | collective-permute-start | bytes 196616 | tf_op jit(solution)/shard_map/while/body/eval_jaxpr/ppermute | solution.py:31
  58.9 9.5 %collective-permute-start.6 = (f32[1,16,1024]{2,1,0:T(8,128)S(1)}, f32[1,16,1024]{2,1,0:T(8,128)S(1)}, u32[]{:S(2)}, u32[]{:S(2)}) collective-permute-start(f32[1,16,1024]{2,1,0:T(8,128)S(1)} %get-tuple-element.528), channel_id=1, source_target_pairs={{0,1},{1,2},{2,3},{3,4},{4,5},{5,6},{6,7},{7,8},{8,9},{9,10},{10,1... | collective-permute-start | bytes 196616 | tf_op jit(solution)/shard_map/while/body/eval_jaxpr/ppermute | solution.py:28
  70.1 9.8 %collective-permute-start.5 = (f32[1,16,1024]{2,1,0:T(8,128)S(1)}, f32[1,16,1024]{2,1,0:T(8,128)S(1)}, u32[]{:S(2)}, u32[]{:S(2)}) collective-permute-start(f32[1,16,1024]{2,1,0:T(8,128)S(1)} %get-tuple-element.527), channel_id=1, source_target_pairs={{1,0},{2,1},{3,2},{4,3},{5,4},{6,5},{7,6},{8,7},{9,8},{10,9},{11,1... | collective-permute-start | bytes 196616 | tf_op jit(solution)/shard_map/while/body/eval_jaxpr/ppermute | solution.py:31
  72.1 9.5 %collective-permute-start.6 = (f32[1,16,1024]{2,1,0:T(8,128)S(1)}, f32[1,16,1024]{2,1,0:T(8,128)S(1)}, u32[]{:S(2)}, u32[]{:S(2)}) collective-permute-start(f32[1,16,1024]{2,1,0:T(8,128)S(1)} %get-tuple-element.528), channel_id=1, source_target_pairs={{0,1},{1,2},{2,3},{3,4},{4,5},{5,6},{6,7},{7,8},{8,9},{9,10},{10,1... | collective-permute-start | bytes 196616 | tf_op jit(solution)/shard_map/while/body/eval_jaxpr/ppermute | solution.py:28
  83.3 9.8 %collective-permute-start.5 = (f32[1,16,1024]{2,1,0:T(8,128)S(1)}, f32[1,16,1024]{2,1,0:T(8,128)S(1)}, u32[]{:S(2)}, u32[]{:S(2)}) collective-permute-start(f32[1,16,1024]{2,1,0:T(8,128)S(1)} %get-tuple-element.527), channel_id=1, source_target_pairs={{1,0},{2,1},{3,2},{4,3},{5,4},{6,5},{7,6},{8,7},{9,8},{10,9},{11,1... | collective-permute-start | bytes 196616 | tf_op jit(solution)/shard_map/while/body/eval_jaxpr/ppermute | solution.py:31
  85.2 9.5 %collective-permute-start.6 = (f32[1,16,1024]{2,1,0:T(8,128)S(1)}, f32[1,16,1024]{2,1,0:T(8,128)S(1)}, u32[]{:S(2)}, u32[]{:S(2)}) collective-permute-start(f32[1,16,1024]{2,1,0:T(8,128)S(1)} %get-tuple-element.528), channel_id=1, source_target_pairs={{0,1},{1,2},{2,3},{3,4},{4,5},{5,6},{6,7},{7,8},{8,9},{9,10},{10,1... | collective-permute-start | bytes 196616 | tf_op jit(solution)/shard_map/while/body/eval_jaxpr/ppermute | solution.py:28
  96.3 68.3 %collective-permute-start.13 = (f32[1,16,1024]{2,1,0:T(8,128)S(1)}, f32[1,16,1024]{2,1,0:T(8,128)S(1)}, u32[]{:S(2)}, u32[]{:S(2)}) collective-permute-start(f32[1,16,1024]{2,1,0:T(8,128)S(1)} %get-tuple-element.409), channel_id=1, source_target_pairs={{1,0},{2,1},{3,2},{4,3},{5,4},{6,5},{7,6},{8,7},{9,8},{10,9},{11,1... | collective-permute-start | bytes 196616 | tf_op jit(solution)/shard_map/ppermute | solution.py:31
  98.3 66.4 %collective-permute-start.14 = (f32[1,16,1024]{2,1,0:T(8,128)S(1)}, f32[1,16,1024]{2,1,0:T(8,128)S(1)}, u32[]{:S(2)}, u32[]{:S(2)}) collective-permute-start(f32[1,16,1024]{2,1,0:T(8,128)S(1)} %get-tuple-element.408), channel_id=1, source_target_pairs={{0,1},{1,2},{2,3},{3,4},{4,5},{5,6},{6,7},{7,8},{8,9},{9,10},{10,1... | collective-permute-start | bytes 196616 | tf_op jit(solution)/shard_map/ppermute | solution.py:28
  165.9 15.7 %collective-permute-start.15 = (f32[4,1,16,1024]{3,2,1,0:T(8,128)S(1)}, f32[4,1,16,1024]{3,2,1,0:T(8,128)S(1)}, u32[]{:S(2)}, u32[]{:S(2)}) collective-permute-start(f32[4,1,16,1024]{3,2,1,0:T(8,128)S(1)} %get-tuple-element.384), channel_id=1, source_target_pairs={{0,1},{1,2},{2,3},{3,4},{4,5},{5,6},{6,7},{7,8},{8,9},{9,10},{10,1... | collective-permute-start | bytes 786440 | tf_op jit(solution)/shard_map/ppermute | solution.py:28
  169.8 11.8 %collective-permute-start.16 = (f32[4,1,16,1024]{3,2,1,0:T(8,128)S(1)}, f32[4,1,16,1024]{3,2,1,0:T(8,128)S(1)}, u32[]{:S(2)}, u32[]{:S(2)}) collective-permute-start(f32[4,1,16,1024]{3,2,1,0:T(8,128)S(1)} %get-tuple-element.385), channel_id=1, source_target_pairs={{1,0},{2,1},{3,2},{4,3},{5,4},{6,5},{7,6},{8,7},{9,8},{10,9},{11,1... | collective-permute-start | bytes 786440 | tf_op jit(solution)/shard_map/ppermute | solution.py:31
  172.0 18.7 %collective-permute-start.21 = (f32[4,1,4,256]{3,2,0,1:T(4,128)S(1)}, f32[4,1,4,256]{3,2,0,1:T(4,128)S(1)}, u32[]{:S(2)}, u32[]{:S(2)}) collective-permute-start(f32[4,1,4,256]{3,2,0,1:T(4,128)S(1)} %multiply_bitcast_fusion), channel_id=1, source_target_pairs={{1,0},{2,1},{3,2},{4,3},{5,4},{6,5},{7,6},{8,7},{9,8},{10,9},{11,1... | collective-permute-start | bytes 49160 | tf_op jit(solution)/shard_map/ppermute | solution.py:31
  173.9 16.8 %collective-permute-start.22 = (f32[4,1,4,256]{3,2,0,1:T(4,128)S(1)}, f32[4,1,4,256]{3,2,0,1:T(4,128)S(1)}, u32[]{:S(2)}, u32[]{:S(2)}) collective-permute-start(f32[4,1,4,256]{3,2,0,1:T(4,128)S(1)} %multiply_bitcast_fusion), channel_id=1, source_target_pairs={{0,1},{1,2},{2,3},{3,4},{4,5},{5,6},{6,7},{7,8},{8,9},{9,10},{10,1... | collective-permute-start | bytes 49160 | tf_op jit(solution)/shard_map/ppermute | solution.py:28
  184.9 15.3 %collective-permute-start.17 = (f32[4,1,16,1024]{3,2,1,0:T(8,128)S(1)}, f32[4,1,16,1024]{3,2,1,0:T(8,128)S(1)}, u32[]{:S(2)}, u32[]{:S(2)}) collective-permute-start(f32[4,1,16,1024]{3,2,1,0:T(8,128)S(1)} %get-tuple-element.382), channel_id=1, source_target_pairs={{0,1},{1,2},{2,3},{3,4},{4,5},{5,6},{6,7},{7,8},{8,9},{9,10},{10,1... | collective-permute-start | bytes 786440 | tf_op jit(solution)/shard_map/ppermute | solution.py:28
  188.8 11.7 %collective-permute-start.18 = (f32[4,1,16,1024]{3,2,1,0:T(8,128)S(1)}, f32[4,1,16,1024]{3,2,1,0:T(8,128)S(1)}, u32[]{:S(2)}, u32[]{:S(2)}) collective-permute-start(f32[4,1,16,1024]{3,2,1,0:T(8,128)S(1)} %get-tuple-element.383), channel_id=1, source_target_pairs={{1,0},{2,1},{3,2},{4,3},{5,4},{6,5},{7,6},{8,7},{9,8},{10,9},{11,1... | collective-permute-start | bytes 786440 | tf_op jit(solution)/shard_map/ppermute | solution.py:31
  191.0 69.5 %collective-permute-start.23 = (f32[4,1,4,256]{3,2,0,1:T(4,128)S(1)}, f32[4,1,4,256]{3,2,0,1:T(4,128)S(1)}, u32[]{:S(2)}, u32[]{:S(2)}) collective-permute-start(f32[4,1,4,256]{3,2,0,1:T(4,128)S(1)} %fusion.164), channel_id=1, source_target_pairs={{1,0},{2,1},{3,2},{4,3},{5,4},{6,5},{7,6},{8,7},{9,8},{10,9},{11,1... | collective-permute-start | bytes 49160 | tf_op jit(solution)/shard_map/ppermute | solution.py:31
  192.9 67.6 %collective-permute-start.24 = (f32[4,1,4,256]{3,2,0,1:T(4,128)S(1)}, f32[4,1,4,256]{3,2,0,1:T(4,128)S(1)}, u32[]{:S(2)}, u32[]{:S(2)}) collective-permute-start(f32[4,1,4,256]{3,2,0,1:T(4,128)S(1)} %fusion.164), channel_id=1, source_target_pairs={{0,1},{1,2},{2,3},{3,4},{4,5},{5,6},{6,7},{7,8},{8,9},{9,10},{10,1... | collective-permute-start | bytes 49160 | tf_op jit(solution)/shard_map/ppermute | solution.py:28
  202.7 9.9 %collective-permute-start.7 = (f32[1,16,1024]{2,1,0:T(8,128)S(1)}, f32[1,16,1024]{2,1,0:T(8,128)S(1)}, u32[]{:S(2)}, u32[]{:S(2)}) collective-permute-start(f32[1,16,1024]{2,1,0:T(8,128)S(1)} %get-tuple-element.537), channel_id=1, source_target_pairs={{1,0},{2,1},{3,2},{4,3},{5,4},{6,5},{7,6},{8,7},{9,8},{10,9},{11,1... | collective-permute-start | bytes 196616 | tf_op jit(solution)/shard_map/while/body/eval_jaxpr/ppermute | solution.py:31
  204.6 9.2 %collective-permute-start.8 = (f32[1,16,1024]{2,1,0:T(8,128)S(1)}, f32[1,16,1024]{2,1,0:T(8,128)S(1)}, u32[]{:S(2)}, u32[]{:S(2)}) collective-permute-start(f32[1,16,1024]{2,1,0:T(8,128)S(1)} %get-tuple-element.538), channel_id=1, source_target_pairs={{0,1},{1,2},{2,3},{3,4},{4,5},{5,6},{6,7},{7,8},{8,9},{9,10},{10,1... | collective-permute-start | bytes 196616 | tf_op jit(solution)/shard_map/while/body/eval_jaxpr/ppermute | solution.py:28
  214.5 9.9 %collective-permute-start.7 = (f32[1,16,1024]{2,1,0:T(8,128)S(1)}, f32[1,16,1024]{2,1,0:T(8,128)S(1)}, u32[]{:S(2)}, u32[]{:S(2)}) collective-permute-start(f32[1,16,1024]{2,1,0:T(8,128)S(1)} %get-tuple-element.537), channel_id=1, source_target_pairs={{1,0},{2,1},{3,2},{4,3},{5,4},{6,5},{7,6},{8,7},{9,8},{10,9},{11,1... | collective-permute-start | bytes 196616 | tf_op jit(solution)/shard_map/while/body/eval_jaxpr/ppermute | solution.py:31
  216.4 9.6 %collective-permute-start.8 = (f32[1,16,1024]{2,1,0:T(8,128)S(1)}, f32[1,16,1024]{2,1,0:T(8,128)S(1)}, u32[]{:S(2)}, u32[]{:S(2)}) collective-permute-start(f32[1,16,1024]{2,1,0:T(8,128)S(1)} %get-tuple-element.538), channel_id=1, source_target_pairs={{0,1},{1,2},{2,3},{3,4},{4,5},{5,6},{6,7},{7,8},{8,9},{9,10},{10,1... | collective-permute-start | bytes 196616 | tf_op jit(solution)/shard_map/while/body/eval_jaxpr/ppermute | solution.py:28
  226.7 9.8 %collective-permute-start.7 = (f32[1,16,1024]{2,1,0:T(8,128)S(1)}, f32[1,16,1024]{2,1,0:T(8,128)S(1)}, u32[]{:S(2)}, u32[]{:S(2)}) collective-permute-start(f32[1,16,1024]{2,1,0:T(8,128)S(1)} %get-tuple-element.537), channel_id=1, source_target_pairs={{1,0},{2,1},{3,2},{4,3},{5,4},{6,5},{7,6},{8,7},{9,8},{10,9},{11,1... | collective-permute-start | bytes 196616 | tf_op jit(solution)/shard_map/while/body/eval_jaxpr/ppermute | solution.py:31
  228.7 9.5 %collective-permute-start.8 = (f32[1,16,1024]{2,1,0:T(8,128)S(1)}, f32[1,16,1024]{2,1,0:T(8,128)S(1)}, u32[]{:S(2)}, u32[]{:S(2)}) collective-permute-start(f32[1,16,1024]{2,1,0:T(8,128)S(1)} %get-tuple-element.538), channel_id=1, source_target_pairs={{0,1},{1,2},{2,3},{3,4},{4,5},{5,6},{6,7},{7,8},{8,9},{9,10},{10,1... | collective-permute-start | bytes 196616 | tf_op jit(solution)/shard_map/while/body/eval_jaxpr/ppermute | solution.py:28
  238.9 9.8 %collective-permute-start.7 = (f32[1,16,1024]{2,1,0:T(8,128)S(1)}, f32[1,16,1024]{2,1,0:T(8,128)S(1)}, u32[]{:S(2)}, u32[]{:S(2)}) collective-permute-start(f32[1,16,1024]{2,1,0:T(8,128)S(1)} %get-tuple-element.537), channel_id=1, source_target_pairs={{1,0},{2,1},{3,2},{4,3},{5,4},{6,5},{7,6},{8,7},{9,8},{10,9},{11,1... | collective-permute-start | bytes 196616 | tf_op jit(solution)/shard_map/while/body/eval_jaxpr/ppermute | solution.py:31
  240.8 9.5 %collective-permute-start.8 = (f32[1,16,1024]{2,1,0:T(8,128)S(1)}, f32[1,16,1024]{2,1,0:T(8,128)S(1)}, u32[]{:S(2)}, u32[]{:S(2)}) collective-permute-start(f32[1,16,1024]{2,1,0:T(8,128)S(1)} %get-tuple-element.538), channel_id=1, source_target_pairs={{0,1},{1,2},{2,3},{3,4},{4,5},{5,6},{6,7},{7,8},{8,9},{9,10},{10,1... | collective-permute-start | bytes 196616 | tf_op jit(solution)/shard_map/while/body/eval_jaxpr/ppermute | solution.py:28
  250.9 25.0 %collective-permute-start.19 = (f32[1,16,1024]{2,1,0:T(8,128)S(1)}, f32[1,16,1024]{2,1,0:T(8,128)S(1)}, u32[]{:S(2)}, u32[]{:S(2)}) collective-permute-start(f32[1,16,1024]{2,1,0:T(8,128)S(1)} %get-tuple-element.407), channel_id=1, source_target_pairs={{1,0},{2,1},{3,2},{4,3},{5,4},{6,5},{7,6},{8,7},{9,8},{10,9},{11,1... | collective-permute-start | bytes 196616 | tf_op jit(solution)/shard_map/ppermute | solution.py:31
  252.9 23.0 %collective-permute-start.20 = (f32[1,16,1024]{2,1,0:T(8,128)S(1)}, f32[1,16,1024]{2,1,0:T(8,128)S(1)}, u32[]{:S(2)}, u32[]{:S(2)}) collective-permute-start(f32[1,16,1024]{2,1,0:T(8,128)S(1)} %get-tuple-element.406), channel_id=1, source_target_pairs={{0,1},{1,2},{2,3},{3,4},{4,5},{5,6},{6,7},{7,8},{8,9},{9,10},{10,1... | collective-permute-start | bytes 196616 | tf_op jit(solution)/shard_map/ppermute | solution.py:28
  319.6 9.2 %collective-permute-start = (f32[4,1,4,256]{3,2,1,0:T(4,128)S(1)}, f32[4,1,4,256]{3,2,1,0:T(4,128)S(1)}, u32[]{:S(2)}, u32[]{:S(2)}) collective-permute-start(f32[4,1,4,256]{3,2,1,0:T(4,128)S(1)} %get-tuple-element.605), channel_id=1, source_target_pairs={{1,0},{2,1},{3,2},{4,3},{5,4},{6,5},{7,6},{8,7},{9,8},{10,9},{11,1... | collective-permute-start | bytes 49160 | tf_op jit(solution)/shard_map/while/body/eval_jaxpr/ppermute | solution.py:31
  321.5 8.7 %collective-permute-start.1 = (f32[4,1,4,256]{3,2,1,0:T(4,128)S(1)}, f32[4,1,4,256]{3,2,1,0:T(4,128)S(1)}, u32[]{:S(2)}, u32[]{:S(2)}) collective-permute-start(f32[4,1,4,256]{3,2,1,0:T(4,128)S(1)} %get-tuple-element.605), channel_id=1, source_target_pairs={{0,1},{1,2},{2,3},{3,4},{4,5},{5,6},{6,7},{7,8},{8,9},{9,10},{10,1... | collective-permute-start | bytes 49160 | tf_op jit(solution)/shard_map/while/body/eval_jaxpr/ppermute | solution.py:28
  330.4 9.5 %collective-permute-start.2 = (f32[4,1,4,256]{3,2,1,0:T(4,128)S(1)}, f32[4,1,4,256]{3,2,1,0:T(4,128)S(1)}, u32[]{:S(2)}, u32[]{:S(2)}) collective-permute-start(f32[4,1,4,256]{3,2,1,0:T(4,128)S(1)} %fusion.179), channel_id=1, source_target_pairs={{1,0},{2,1},{3,2},{4,3},{5,4},{6,5},{7,6},{8,7},{9,8},{10,9},{11,1... | collective-permute-start | bytes 49160 | tf_op jit(solution)/shard_map/while/body/eval_jaxpr/ppermute | solution.py:31
  332.3 9.0 %collective-permute-start.3 = (f32[4,1,4,256]{3,2,1,0:T(4,128)S(1)}, f32[4,1,4,256]{3,2,1,0:T(4,128)S(1)}, u32[]{:S(2)}, u32[]{:S(2)}) collective-permute-start(f32[4,1,4,256]{3,2,1,0:T(4,128)S(1)} %fusion.179), channel_id=1, source_target_pairs={{0,1},{1,2},{2,3},{3,4},{4,5},{5,6},{6,7},{7,8},{8,9},{9,10},{10,1... | collective-permute-start | bytes 49160 | tf_op jit(solution)/shard_map/while/body/eval_jaxpr/ppermute | solution.py:28
  346.6 9.5 %collective-permute-start = (f32[4,1,4,256]{3,2,1,0:T(4,128)S(1)}, f32[4,1,4,256]{3,2,1,0:T(4,128)S(1)}, u32[]{:S(2)}, u32[]{:S(2)}) collective-permute-start(f32[4,1,4,256]{3,2,1,0:T(4,128)S(1)} %get-tuple-element.605), channel_id=1, source_target_pairs={{1,0},{2,1},{3,2},{4,3},{5,4},{6,5},{7,6},{8,7},{9,8},{10,9},{11,1... | collective-permute-start | bytes 49160 | tf_op jit(solution)/shard_map/while/body/eval_jaxpr/ppermute | solution.py:31
  348.5 9.0 %collective-permute-start.1 = (f32[4,1,4,256]{3,2,1,0:T(4,128)S(1)}, f32[4,1,4,256]{3,2,1,0:T(4,128)S(1)}, u32[]{:S(2)}, u32[]{:S(2)}) collective-permute-start(f32[4,1,4,256]{3,2,1,0:T(4,128)S(1)} %get-tuple-element.605), channel_id=1, source_target_pairs={{0,1},{1,2},{2,3},{3,4},{4,5},{5,6},{6,7},{7,8},{8,9},{9,10},{10,1... | collective-permute-start | bytes 49160 | tf_op jit(solution)/shard_map/while/body/eval_jaxpr/ppermute | solution.py:28
  357.7 9.5 %collective-permute-start.2 = (f32[4,1,4,256]{3,2,1,0:T(4,128)S(1)}, f32[4,1,4,256]{3,2,1,0:T(4,128)S(1)}, u32[]{:S(2)}, u32[]{:S(2)}) collective-permute-start(f32[4,1,4,256]{3,2,1,0:T(4,128)S(1)} %fusion.179), channel_id=1, source_target_pairs={{1,0},{2,1},{3,2},{4,3},{5,4},{6,5},{7,6},{8,7},{9,8},{10,9},{11,1... | collective-permute-start | bytes 49160 | tf_op jit(solution)/shard_map/while/body/eval_jaxpr/ppermute | solution.py:31
  359.6 9.0 %collective-permute-start.3 = (f32[4,1,4,256]{3,2,1,0:T(4,128)S(1)}, f32[4,1,4,256]{3,2,1,0:T(4,128)S(1)}, u32[]{:S(2)}, u32[]{:S(2)}) collective-permute-start(f32[4,1,4,256]{3,2,1,0:T(4,128)S(1)} %fusion.179), channel_id=1, source_target_pairs={{0,1},{1,2},{2,3},{3,4},{4,5},{5,6},{6,7},{7,8},{8,9},{9,10},{10,1... | collective-permute-start | bytes 49160 | tf_op jit(solution)/shard_map/while/body/eval_jaxpr/ppermute | solution.py:28
  373.8 9.5 %collective-permute-start = (f32[4,1,4,256]{3,2,1,0:T(4,128)S(1)}, f32[4,1,4,256]{3,2,1,0:T(4,128)S(1)}, u32[]{:S(2)}, u32[]{:S(2)}) collective-permute-start(f32[4,1,4,256]{3,2,1,0:T(4,128)S(1)} %get-tuple-element.605), channel_id=1, source_target_pairs={{1,0},{2,1},{3,2},{4,3},{5,4},{6,5},{7,6},{8,7},{9,8},{10,9},{11,1... | collective-permute-start | bytes 49160 | tf_op jit(solution)/shard_map/while/body/eval_jaxpr/ppermute | solution.py:31
  375.8 9.0 %collective-permute-start.1 = (f32[4,1,4,256]{3,2,1,0:T(4,128)S(1)}, f32[4,1,4,256]{3,2,1,0:T(4,128)S(1)}, u32[]{:S(2)}, u32[]{:S(2)}) collective-permute-start(f32[4,1,4,256]{3,2,1,0:T(4,128)S(1)} %get-tuple-element.605), channel_id=1, source_target_pairs={{0,1},{1,2},{2,3},{3,4},{4,5},{5,6},{6,7},{7,8},{8,9},{9,10},{10,1... | collective-permute-start | bytes 49160 | tf_op jit(solution)/shard_map/while/body/eval_jaxpr/ppermute | solution.py:28
  384.9 9.5 %collective-permute-start.2 = (f32[4,1,4,256]{3,2,1,0:T(4,128)S(1)}, f32[4,1,4,256]{3,2,1,0:T(4,128)S(1)}, u32[]{:S(2)}, u32[]{:S(2)}) collective-permute-start(f32[4,1,4,256]{3,2,1,0:T(4,128)S(1)} %fusion.179), channel_id=1, source_target_pairs={{1,0},{2,1},{3,2},{4,3},{5,4},{6,5},{7,6},{8,7},{9,8},{10,9},{11,1... | collective-permute-start | bytes 49160 | tf_op jit(solution)/shard_map/while/body/eval_jaxpr/ppermute | solution.py:31
  386.9 9.0 %collective-permute-start.3 = (f32[4,1,4,256]{3,2,1,0:T(4,128)S(1)}, f32[4,1,4,256]{3,2,1,0:T(4,128)S(1)}, u32[]{:S(2)}, u32[]{:S(2)}) collective-permute-start(f32[4,1,4,256]{3,2,1,0:T(4,128)S(1)} %fusion.179), channel_id=1, source_target_pairs={{0,1},{1,2},{2,3},{3,4},{4,5},{5,6},{6,7},{7,8},{8,9},{9,10},{10,1... | collective-permute-start | bytes 49160 | tf_op jit(solution)/shard_map/while/body/eval_jaxpr/ppermute | solution.py:28
  401.1 9.5 %collective-permute-start = (f32[4,1,4,256]{3,2,1,0:T(4,128)S(1)}, f32[4,1,4,256]{3,2,1,0:T(4,128)S(1)}, u32[]{:S(2)}, u32[]{:S(2)}) collective-permute-start(f32[4,1,4,256]{3,2,1,0:T(4,128)S(1)} %get-tuple-element.605), channel_id=1, source_target_pairs={{1,0},{2,1},{3,2},{4,3},{5,4},{6,5},{7,6},{8,7},{9,8},{10,9},{11,1... | collective-permute-start | bytes 49160 | tf_op jit(solution)/shard_map/while/body/eval_jaxpr/ppermute | solution.py:31
  403.0 9.0 %collective-permute-start.1 = (f32[4,1,4,256]{3,2,1,0:T(4,128)S(1)}, f32[4,1,4,256]{3,2,1,0:T(4,128)S(1)}, u32[]{:S(2)}, u32[]{:S(2)}) collective-permute-start(f32[4,1,4,256]{3,2,1,0:T(4,128)S(1)} %get-tuple-element.605), channel_id=1, source_target_pairs={{0,1},{1,2},{2,3},{3,4},{4,5},{5,6},{6,7},{7,8},{8,9},{9,10},{10,1... | collective-permute-start | bytes 49160 | tf_op jit(solution)/shard_map/while/body/eval_jaxpr/ppermute | solution.py:28
  412.2 9.5 %collective-permute-start.2 = (f32[4,1,4,256]{3,2,1,0:T(4,128)S(1)}, f32[4,1,4,256]{3,2,1,0:T(4,128)S(1)}, u32[]{:S(2)}, u32[]{:S(2)}) collective-permute-start(f32[4,1,4,256]{3,2,1,0:T(4,128)S(1)} %fusion.179), channel_id=1, source_target_pairs={{1,0},{2,1},{3,2},{4,3},{5,4},{6,5},{7,6},{8,7},{9,8},{10,9},{11,1... | collective-permute-start | bytes 49160 | tf_op jit(solution)/shard_map/while/body/eval_jaxpr/ppermute | solution.py:31
  414.1 9.0 %collective-permute-start.3 = (f32[4,1,4,256]{3,2,1,0:T(4,128)S(1)}, f32[4,1,4,256]{3,2,1,0:T(4,128)S(1)}, u32[]{:S(2)}, u32[]{:S(2)}) collective-permute-start(f32[4,1,4,256]{3,2,1,0:T(4,128)S(1)} %fusion.179), channel_id=1, source_target_pairs={{0,1},{1,2},{2,3},{3,4},{4,5},{5,6},{6,7},{7,8},{8,9},{9,10},{10,1... | collective-permute-start | bytes 49160 | tf_op jit(solution)/shard_map/while/body/eval_jaxpr/ppermute | solution.py:28
  428.3 9.5 %collective-permute-start = (f32[4,1,4,256]{3,2,1,0:T(4,128)S(1)}, f32[4,1,4,256]{3,2,1,0:T(4,128)S(1)}, u32[]{:S(2)}, u32[]{:S(2)}) collective-permute-start(f32[4,1,4,256]{3,2,1,0:T(4,128)S(1)} %get-tuple-element.605), channel_id=1, source_target_pairs={{1,0},{2,1},{3,2},{4,3},{5,4},{6,5},{7,6},{8,7},{9,8},{10,9},{11,1... | collective-permute-start | bytes 49160 | tf_op jit(solution)/shard_map/while/body/eval_jaxpr/ppermute | solution.py:31
  430.3 9.0 %collective-permute-start.1 = (f32[4,1,4,256]{3,2,1,0:T(4,128)S(1)}, f32[4,1,4,256]{3,2,1,0:T(4,128)S(1)}, u32[]{:S(2)}, u32[]{:S(2)}) collective-permute-start(f32[4,1,4,256]{3,2,1,0:T(4,128)S(1)} %get-tuple-element.605), channel_id=1, source_target_pairs={{0,1},{1,2},{2,3},{3,4},{4,5},{5,6},{6,7},{7,8},{8,9},{9,10},{10,1... | collective-permute-start | bytes 49160 | tf_op jit(solution)/shard_map/while/body/eval_jaxpr/ppermute | solution.py:28
  439.4 9.5 %collective-permute-start.2 = (f32[4,1,4,256]{3,2,1,0:T(4,128)S(1)}, f32[4,1,4,256]{3,2,1,0:T(4,128)S(1)}, u32[]{:S(2)}, u32[]{:S(2)}) collective-permute-start(f32[4,1,4,256]{3,2,1,0:T(4,128)S(1)} %fusion.179), channel_id=1, source_target_pairs={{1,0},{2,1},{3,2},{4,3},{5,4},{6,5},{7,6},{8,7},{9,8},{10,9},{11,1... | collective-permute-start | bytes 49160 | tf_op jit(solution)/shard_map/while/body/eval_jaxpr/ppermute | solution.py:31
  441.4 9.0 %collective-permute-start.3 = (f32[4,1,4,256]{3,2,1,0:T(4,128)S(1)}, f32[4,1,4,256]{3,2,1,0:T(4,128)S(1)}, u32[]{:S(2)}, u32[]{:S(2)}) collective-permute-start(f32[4,1,4,256]{3,2,1,0:T(4,128)S(1)} %fusion.179), channel_id=1, source_target_pairs={{0,1},{1,2},{2,3},{3,4},{4,5},{5,6},{6,7},{7,8},{8,9},{9,10},{10,1... | collective-permute-start | bytes 49160 | tf_op jit(solution)/shard_map/while/body/eval_jaxpr/ppermute | solution.py:28
  455.6 9.5 %collective-permute-start = (f32[4,1,4,256]{3,2,1,0:T(4,128)S(1)}, f32[4,1,4,256]{3,2,1,0:T(4,128)S(1)}, u32[]{:S(2)}, u32[]{:S(2)}) collective-permute-start(f32[4,1,4,256]{3,2,1,0:T(4,128)S(1)} %get-tuple-element.605), channel_id=1, source_target_pairs={{1,0},{2,1},{3,2},{4,3},{5,4},{6,5},{7,6},{8,7},{9,8},{10,9},{11,1... | collective-permute-start | bytes 49160 | tf_op jit(solution)/shard_map/while/body/eval_jaxpr/ppermute | solution.py:31
  457.5 9.0 %collective-permute-start.1 = (f32[4,1,4,256]{3,2,1,0:T(4,128)S(1)}, f32[4,1,4,256]{3,2,1,0:T(4,128)S(1)}, u32[]{:S(2)}, u32[]{:S(2)}) collective-permute-start(f32[4,1,4,256]{3,2,1,0:T(4,128)S(1)} %get-tuple-element.605), channel_id=1, source_target_pairs={{0,1},{1,2},{2,3},{3,4},{4,5},{5,6},{6,7},{7,8},{8,9},{9,10},{10,1... | collective-permute-start | bytes 49160 | tf_op jit(solution)/shard_map/while/body/eval_jaxpr/ppermute | solution.py:28
  466.7 9.5 %collective-permute-start.2 = (f32[4,1,4,256]{3,2,1,0:T(4,128)S(1)}, f32[4,1,4,256]{3,2,1,0:T(4,128)S(1)}, u32[]{:S(2)}, u32[]{:S(2)}) collective-permute-start(f32[4,1,4,256]{3,2,1,0:T(4,128)S(1)} %fusion.179), channel_id=1, source_target_pairs={{1,0},{2,1},{3,2},{4,3},{5,4},{6,5},{7,6},{8,7},{9,8},{10,9},{11,1... | collective-permute-start | bytes 49160 | tf_op jit(solution)/shard_map/while/body/eval_jaxpr/ppermute | solution.py:31
  468.6 9.0 %collective-permute-start.3 = (f32[4,1,4,256]{3,2,1,0:T(4,128)S(1)}, f32[4,1,4,256]{3,2,1,0:T(4,128)S(1)}, u32[]{:S(2)}, u32[]{:S(2)}) collective-permute-start(f32[4,1,4,256]{3,2,1,0:T(4,128)S(1)} %fusion.179), channel_id=1, source_target_pairs={{0,1},{1,2},{2,3},{3,4},{4,5},{5,6},{6,7},{7,8},{8,9},{9,10},{10,1... | collective-permute-start | bytes 49160 | tf_op jit(solution)/shard_map/while/body/eval_jaxpr/ppermute | solution.py:28
  482.9 9.5 %collective-permute-start = (f32[4,1,4,256]{3,2,1,0:T(4,128)S(1)}, f32[4,1,4,256]{3,2,1,0:T(4,128)S(1)}, u32[]{:S(2)}, u32[]{:S(2)}) collective-permute-start(f32[4,1,4,256]{3,2,1,0:T(4,128)S(1)} %get-tuple-element.605), channel_id=1, source_target_pairs={{1,0},{2,1},{3,2},{4,3},{5,4},{6,5},{7,6},{8,7},{9,8},{10,9},{11,1... | collective-permute-start | bytes 49160 | tf_op jit(solution)/shard_map/while/body/eval_jaxpr/ppermute | solution.py:31
  484.8 9.0 %collective-permute-start.1 = (f32[4,1,4,256]{3,2,1,0:T(4,128)S(1)}, f32[4,1,4,256]{3,2,1,0:T(4,128)S(1)}, u32[]{:S(2)}, u32[]{:S(2)}) collective-permute-start(f32[4,1,4,256]{3,2,1,0:T(4,128)S(1)} %get-tuple-element.605), channel_id=1, source_target_pairs={{0,1},{1,2},{2,3},{3,4},{4,5},{5,6},{6,7},{7,8},{8,9},{9,10},{10,1... | collective-permute-start | bytes 49160 | tf_op jit(solution)/shard_map/while/body/eval_jaxpr/ppermute | solution.py:28
  494.0 9.5 %collective-permute-start.2 = (f32[4,1,4,256]{3,2,1,0:T(4,128)S(1)}, f32[4,1,4,256]{3,2,1,0:T(4,128)S(1)}, u32[]{:S(2)}, u32[]{:S(2)}) collective-permute-start(f32[4,1,4,256]{3,2,1,0:T(4,128)S(1)} %fusion.179), channel_id=1, source_target_pairs={{1,0},{2,1},{3,2},{4,3},{5,4},{6,5},{7,6},{8,7},{9,8},{10,9},{11,1... | collective-permute-start | bytes 49160 | tf_op jit(solution)/shard_map/while/body/eval_jaxpr/ppermute | solution.py:31
  495.9 9.0 %collective-permute-start.3 = (f32[4,1,4,256]{3,2,1,0:T(4,128)S(1)}, f32[4,1,4,256]{3,2,1,0:T(4,128)S(1)}, u32[]{:S(2)}, u32[]{:S(2)}) collective-permute-start(f32[4,1,4,256]{3,2,1,0:T(4,128)S(1)} %fusion.179), channel_id=1, source_target_pairs={{0,1},{1,2},{2,3},{3,4},{4,5},{5,6},{6,7},{7,8},{8,9},{9,10},{10,1... | collective-permute-start | bytes 49160 | tf_op jit(solution)/shard_map/while/body/eval_jaxpr/ppermute | solution.py:28
  510.1 9.5 %collective-permute-start.25 = (f32[4,1,4,256]{3,2,1,0:T(4,128)S(1)}, f32[4,1,4,256]{3,2,1,0:T(4,128)S(1)}, u32[]{:S(2)}, u32[]{:S(2)}) collective-permute-start(f32[4,1,4,256]{3,2,1,0:T(4,128)S(1)} %get-tuple-element.259), channel_id=1, source_target_pairs={{1,0},{2,1},{3,2},{4,3},{5,4},{6,5},{7,6},{8,7},{9,8},{10,9},{11,1... | collective-permute-start | bytes 49160 | tf_op jit(solution)/shard_map/ppermute | solution.py:31
  512.0 9.0 %collective-permute-start.26 = (f32[4,1,4,256]{3,2,1,0:T(4,128)S(1)}, f32[4,1,4,256]{3,2,1,0:T(4,128)S(1)}, u32[]{:S(2)}, u32[]{:S(2)}) collective-permute-start(f32[4,1,4,256]{3,2,1,0:T(4,128)S(1)} %get-tuple-element.259), channel_id=1, source_target_pairs={{0,1},{1,2},{2,3},{3,4},{4,5},{5,6},{6,7},{7,8},{8,9},{9,10},{10,1... | collective-permute-start | bytes 49160 | tf_op jit(solution)/shard_map/ppermute | solution.py:28
  521.2 9.5 %collective-permute-start.27 = (f32[4,1,4,256]{3,2,0,1:T(4,128)S(1)}, f32[4,1,4,256]{3,2,0,1:T(4,128)S(1)}, u32[]{:S(2)}, u32[]{:S(2)}) collective-permute-start(f32[4,1,4,256]{3,2,0,1:T(4,128)S(1)} %bitcast.123), channel_id=1, source_target_pairs={{1,0},{2,1},{3,2},{4,3},{5,4},{6,5},{7,6},{8,7},{9,8},{10,9},{11,1... | collective-permute-start | bytes 49160 | tf_op jit(solution)/shard_map/ppermute | solution.py:31
  523.1 9.0 %collective-permute-start.28 = (f32[4,1,4,256]{3,2,0,1:T(4,128)S(1)}, f32[4,1,4,256]{3,2,0,1:T(4,128)S(1)}, u32[]{:S(2)}, u32[]{:S(2)}) collective-permute-start(f32[4,1,4,256]{3,2,0,1:T(4,128)S(1)} %bitcast.124), channel_id=1, source_target_pairs={{0,1},{1,2},{2,3},{3,4},{4,5},{5,6},{6,7},{7,8},{8,9},{9,10},{10,1... | collective-permute-start | bytes 49160 | tf_op jit(solution)/shard_map/ppermute | solution.py:28
  (15 other events, 88.3 us)
where the time goes:
time: 552 us; the launch traced here: 546 us
  starting transfers between devices  308 us (56%)
  local copies, waits for them, and re-layouts  132 us (24%)
  waiting for transfers between devices  73.9 us (13%)
  other arithmetic  30 us (5%)
    ppermute x32, starting transfers between devices, padded_2(): lax.ppermute(lax.slice_in_dim(block, block.shape[dim] - width, None, axis...  232 us
    ppermute x32, starting transfers between devices, padded_2(): lax.ppermute(lax.slice_in_dim(block, 0, width, axis=dim), axis, backward)  62.1 us
    concatenate x4, local copies, waits for them, and re-layouts, fine_step(): stacked = jnp.concatenate([fraction[None], velocity])  58.8 us
    concatenate x4, local copies, waits for them, and re-layouts, shards(): fine_end = jnp.concatenate([fraction[None], velocity])  57.4 us
    ppermute x32, waiting for transfers between devices, padded_2(): lax.ppermute(lax.slice_in_dim(block, block.shape[dim] - width, None, axis...  38.5 us
    ppermute x7, waiting for transfers between devices, shifted(): return lax.ppermute(value, axis, pairs)  21.9 us
    ppermute x32, waiting for transfers between devices, padded_2(): lax.ppermute(lax.slice_in_dim(block, 0, width, axis=dim), axis, backward)  13.6 us
    ppermute x7, starting transfers between devices, shifted(): return lax.ppermute(value, axis, pairs)  13.4 us
  transfers between devices with their start and end apart: 71, of which 44 were waited for; matrix products, arithmetic and copies ran while one was open for 15% of the time, Pallas kernels for 0%

commit v1 on v0

v1 whole, which is shorter than its diff:
```python
import functools

import jax
import jax.numpy as jnp
from jax import lax
from jax.experimental import pallas as pl
from jax.experimental.pallas import tpu as pltpu
from jax.sharding import PartitionSpec as P

MESH = pl.DeviceIdType.MESH
F32 = jnp.float32

ROWS = 4
NZ = 16
SUB, LANE = 8, 128
H = 4
EXT = ROWS + 2 * H
TILE = 32
TILES = 4
STRIPS = 32
FINE = 2
U = 4
BLOCKS = NZ // U

SLICES, SPACE = 8, 32
wall_scale = 1.5 * 0.25 * 0.5
wall_decay = 4.0
level_scale = 1.0 / 1024.0
fraction_spread, velocity_spread = 0.05, 0.15


def lane_ids():
    sub = lax.broadcasted_iota(jnp.int32, (SUB, LANE), 0)
    lane = lax.broadcasted_iota(jnp.int32, (SUB, LANE), 1)
    return sub, lane


def roll(v, by, axis):
    return pltpu.roll(v, by, axis)


def next_y(v, masks, fill=0.0, by=1):
    ax = v.ndim
    r = roll(v, LANE - by, ax - 1)
    q = roll(r, SUB - 1, ax - 2)
    q = jnp.where(masks["last_sub"], fill, q)
    return jnp.where(masks["last_lane"] if by == 1 else masks["last_group"], q, r)


def prev_y(v, masks, fill=0.0, by=1):
    ax = v.ndim
    r = roll(v, by, ax - 1)
    q = roll(r, 1, ax - 2)
    q = jnp.where(masks["first_sub"], fill, q)
    return jnp.where(masks["first_lane"] if by == 1 else masks["first_group"], q, r)


def upwind(lower, upper, speed_lower, speed_upper):
    speed = speed_lower + speed_upper
    return speed * jnp.where(speed > 0.0, lower, upper)


def rho_of(c):
    return 0.1 + 0.9 * jnp.clip(c, 0.0, 1.0)


def kernel(
    lev_ref, vel_ref, plan_ref, ofrac_ref, ovel_ref,
    levb, c_a, c_b, u, pv, gx, gz, gyl, gyu, rt, p1, p_a, p_b, elec, wall,
    cstart, prev, drive, rx1, rx2, rxs, rxq, t1, t2, w0, w1,
    in_sem, out_sem, fs_send, fs_recv, cs_send, cs_recv,
):
    t = lax.axis_index("tm")
    s = lax.axis_index("space")
    sub, lane = lane_ids()
    masks = {
        "last_sub": sub == SUB - 1, "first_sub": sub == 0,
        "last_lane": lane == LANE - 1, "first_lane": lane == 0,
        "last_group": lane >= LANE - 4, "first_group": lane < 4,
    }

    def there(dt, ds):
        return (t + dt >= 0) & (t + dt < SLICES) & (s + ds >= 0) & (s + ds < SPACE)

    has_left, has_right = s > 0, s < SPACE - 1

    loads = []
    for k in range(SUB):
        cols = pl.ds(LANE * k, LANE)
        loads.append(pltpu.make_async_copy(lev_ref.at[0, :, :, cols], levb.at[:, :, k, :], in_sem.at[0, k]))
        for d in range(3):
            loads.append(pltpu.make_async_copy(
                vel_ref.at[0, d, :, :, cols], u.at[d, pl.ds(H, ROWS), pl.ds(1, NZ), k, :], in_sem.at[1 + d, k]))
    for c in loads:
        c.start()

    zero_line = jnp.zeros((SUB, LANE), F32)

    def zero_pads(e, _):
        for ref in (c_a, c_b, p1, p_a, p_b, pv.at[1], u.at[0], u.at[1], u.at[2]):
            ref[e, 0] = zero_line
            ref[e, NZ + 1] = zero_line
        return 0

    lax.fori_loop(0, EXT, zero_pads, 0)

    def zero_rows(first):
        def one(j, _):
            z = 1 + lax.rem(j, NZ)
            e = first + lax.div(j, NZ)
            for ref in (c_a, c_b, p1, u.at[0], u.at[1], u.at[2]):
                ref[e, z] = zero_line
            return 0
        lax.fori_loop(0, H * NZ, one, 0)

    @pl.when(s == 0)
    def _():
        zero_rows(0)

    @pl.when(s == SPACE - 1)
    def _():
        zero_rows(H + ROWS)

    zero_coarse = jnp.zeros((4, SUB, LANE), F32)
    for ref in (cstart, rx1, rx2, rxs, rxq):
        def one_row(j, _, ref=ref):
            ref[j] = zero_coarse
            return 0
        lax.fori_loop(0, ref.shape[0], one_row, 0)

    barrier = pltpu.get_barrier_semaphore()
    groups = [(0, 2)] + [(sign * k, r) for k, r in ((1, 2), (2, 4), (4, 8)) for sign in (1, -1)]
    expected = jnp.int32(0)
    for dt, reach in groups:
        def greet(j, count, dt=dt, reach=reach):
            ds = j - reach
            ok = there(dt, ds)
            if dt == 0:
                ok = ok & (ds != 0)

            @pl.when(ok)
            def _():
                pl.semaphore_signal(barrier, inc=1, device_id=(t + dt, s + ds), device_id_type=MESH)

            return count + ok.astype(jnp.int32)
        expected = lax.fori_loop(0, 2 * reach + 1, greet, expected)

    strip = sub * 4 + lax.div(lane, TILE)
    first_row = s * ROWS
    tiles = [jnp.clip(lax.div(first_row - 1 + TILE, TILE) - 1, 0, TILES - 1), lax.div(first_row, TILE),
             jnp.clip(lax.div(first_row + ROWS, TILE), 0, TILES - 1)]
    for f in range(FINE):
        for j, tile in enumerate(tiles):
            def paint(q, field, f=f, tile=tile):
                return jnp.where(strip == q, plan_ref[f, tile, q].astype(F32), field)
            elec[f, j] = lax.fori_loop(0, STRIPS, paint, zero_line)
    for z in range(NZ):
        wall[z] = jnp.full((SUB, LANE), wall_scale, F32) * jnp.exp(jnp.full((SUB, LANE), -z / wall_decay, F32))

    for k in range(SUB):
        loads[4 * k].wait()

    def to_fraction(j, _):
        i, z = lax.div(j, NZ), lax.rem(j, NZ)
        c_a[H + i, 1 + z] = levb[i, z].astype(F32) * level_scale
        return 0

    lax.fori_loop(0, ROWS * NZ, to_fraction, 0)
    for k in range(SUB):
        for d in range(3):
            loads[4 * k + 1 + d].wait()

    pl.semaphore_wait(barrier, expected)

    def row_copies(entries, base):
        rights, lefts = [], []
        for n, (ref, skip, count) in enumerate(entries):
            first = H + ROWS - skip - count
            rights.append(pltpu.make_async_remote_copy(
                src_ref=ref.at[pl.ds(first, count), pl.ds(1, NZ)],
                dst_ref=ref.at[pl.ds(first - ROWS, count), pl.ds(1, NZ)],
                send_sem=fs_send.at[base + n, 0], recv_sem=fs_recv.at[base + n, 0],
                device_id=(t, s + 1), device_id_type=MESH))
            first = H + skip
            lefts.append(pltpu.make_async_remote_copy(
                src_ref=ref.at[pl.ds(first, count), pl.ds(1, NZ)],
                dst_ref=ref.at[pl.ds(first + ROWS, count), pl.ds(1, NZ)],
                send_sem=fs_send.at[base + n, 1], recv_sem=fs_recv.at[base + n, 1],
                device_id=(t, s - 1), device_id_type=MESH))
        return rights, lefts

    def start(copies):
        rights, lefts = copies

        @pl.when(has_right)
        def _():
            for c in rights:
                c.start()

        @pl.when(has_left)
        def _():
            for c in lefts:
                c.start()

    def landed(copies):
        rights, lefts = copies

        @pl.when(has_left)
        def _():
            for c in rights:
                c.wait_recv()

        @pl.when(has_right)
        def _():
            for c in lefts:
                c.wait_recv()

    def sent(copies):
        rights, lefts = copies

        @pl.when(has_right)
        def _():
            for c in rights:
                c.wait_send()

        @pl.when(has_left)
        def _():
            for c in lefts:
                c.wait_send()

    def coarse_copy(src, dst, reach, dt, base, ds):
        j = reach - ds
        return pltpu.make_async_remote_copy(
            src_ref=src, dst_ref=dst.at[j], send_sem=cs_send.at[base + j], recv_sem=cs_recv.at[base + j],
            device_id=(t + dt, s + ds), device_id_type=MESH)

    def each_target(src, dst, reach, dt, base, action):
        def one(j, _):
            ds = j - reach
            ok = there(dt, ds)
            if dt == 0:
                ok = ok & (ds != 0)

            @pl.when(ok)
            def _():
                c = coarse_copy(src, dst, reach, dt, base, ds)
                c.start() if action == "start" else c.wait_send()

            return 0
        lax.fori_loop(0, 2 * reach + 1, one, 0)

    def each_source(src, dst, reach, dt, base):
        def one(j, _):
            ds = reach - j
            ok = there(-dt, -ds)
            if dt == 0:
                ok = ok & (ds != 0)

            @pl.when(ok)
            def _():
                coarse_copy(src, dst, reach, dt, base, ds).wait_recv()

            return 0
        lax.fori_loop(0, 2 * reach + 1, one, 0)

    def inside(row):
        return ((row >= 0) & (row < SPACE * ROWS)).astype(F32)

    def over(rows, body):
        lo, hi = rows

        def one(j, _):
            body(lo + lax.div(j, BLOCKS), U * lax.rem(j, BLOCKS))
            return 0
        lax.fori_loop(0, (hi - lo) * BLOCKS, one, 0)

    def six(ref, e, z0):
        mid = ref[e, pl.ds(z0, U + 2)]
        return ref[e - 1, pl.ds(z0 + 1, U)], ref[e + 1, pl.ds(z0 + 1, U)], mid

    def advance(c, new_c, f, e, z0, which, full):
        cxm, cxp, cz = six(c, e, z0)
        uxm, uxp, uz = six(u.at[0], e, z0)
        c0, u0 = cz[1:-1], uz[1:-1]
        cym, cyp = prev_y(c0, masks), next_y(c0, masks)
        w = u[1, e, pl.ds(z0, U + 2)]
        v = u[2, e, pl.ds(z0 + 1, U)]
        vm, vp = prev_y(v, masks), next_y(v, masks)
        net = upwind(c0, cxp, u0, uxp) - upwind(cxm, c0, uxm, u0)
        fz = upwind(cz[:-1], cz[1:], w[:-1], w[1:])
        net = net + (fz[1:] - fz[:-1])
        net = net + (upwind(c0, cyp, v, vp) - upwind(cym, c0, vm, v))
        fresh = c0 - 0.125 * net
        pull = elec[f, which] * wall[pl.ds(z0, U)] / rho_of(c0)
        around = uxm + uxp + uz[:-2] + uz[2:] + prev_y(u0, masks) + next_y(u0, masks)
        px = 0.85 * u0 + (0.025 * around + pull * (cxp - cxm))
        if not full:
            keep = inside(first_row + e - H)
            fresh = fresh * keep
            px = px * keep
        new_c[e, pl.ds(z0 + 1, U)] = fresh
        pv[0, e, pl.ds(z0 + 1, U)] = px
        if full:
            wxm, wxp = u[1, e - 1, pl.ds(z0 + 1, U)], u[1, e + 1, pl.ds(z0 + 1, U)]
            w0_ = w[1:-1]
            around = wxm + wxp + w[:-2] + w[2:] + prev_y(w0_, masks) + next_y(w0_, masks)
            pv[1, e, pl.ds(z0 + 1, U)] = 0.85 * w0_ + (0.025 * around + pull * (cz[2:] - cz[:-2]))
            vxm, vxp, vz = six(u.at[2], e, z0)
            around = vxm + vxp + vz[:-2] + vz[2:] + vm + vp
            pv[2, e, pl.ds(z0 + 1, U)] = 0.85 * v + (0.025 * around + pull * (cyp - cym))

    def face_block(new_c, e, z0, top):
        rz = rho_of(new_c[e, pl.ds(z0, U + 2)])
        r0 = rz[1:-1]
        rxm = rho_of(new_c[e - 1, pl.ds(z0 + 1, U)])
        rxp = rho_of(new_c[e + 1, pl.ds(z0 + 1, U)])
        lower = 1.0 / (rxm + r0)
        upper = 1.0 / (rxp + r0)
        gx[e, pl.ds(z0, U)] = lower
        gx[e + 1, pl.ds(z0, U)] = upper
        zface = 1.0 / (rz[:-1] + rz[1:])
        gz[e, pl.ds(z0, U + 1)] = zface
        yl = 1.0 / (r0 + prev_y(r0, masks, 0.1))
        yu = 1.0 / (r0 + next_y(r0, masks, 0.1))
        gyl[e, pl.ds(z0, U)] = yl
        gyu[e, pl.ds(z0, U)] = yu
        total = lower + upper + (zface[:-1] + zface[1:]) + (yl + yu)
        inverse = 1.0 / total
        if not top:
            inverse = inverse * inside(first_row + e - H)
        rt[e, pl.ds(z0, U)] = inverse
        return inverse

    def first_pressure(new_c, e, z0):
        inverse = face_block(new_c, e, z0, True)
        pz = pv[1, e, pl.ds(z0, U + 2)]
        py = pv[2, e, pl.ds(z0 + 1, U)]
        source = pv[0, e + 1, pl.ds(z0 + 1, U)] - pv[0, e - 1, pl.ds(z0 + 1, U)]
        source = source + (pz[2:] - pz[:-2]) + (next_y(py, masks) - prev_y(py, masks))
        p1[e, pl.ds(z0 + 1, U)] = -(source * inverse)

    def sweep(old, new, e, z0):
        pxm, pxp, pz = six(old, e, z0)
        p0 = pz[1:-1]
        zface = gz[e, pl.ds(z0, U + 1)]
        summed = gx[e, pl.ds(z0, U)] * pxm + gx[e + 1, pl.ds(z0, U)] * pxp
        summed = summed + (zface[:-1] * pz[:-2] + zface[1:] * pz[2:])
        summed = summed + (gyl[e, pl.ds(z0, U)] * prev_y(p0, masks) + gyu[e, pl.ds(z0, U)] * next_y(p0, masks))
        new[e, pl.ds(z0 + 1, U)] = p1[e, pl.ds(z0 + 1, U)] + rt[e, pl.ds(z0, U)] * summed

    def project(new_c, e, z0):
        pxm, pxp, pz = six(p_a, e, z0)
        p0 = pz[1:-1]
        scale = 0.125 / rho_of(new_c[e, pl.ds(z0 + 1, U)])
        zs = pl.ds(z0 + 1, U)
        u[0, e, zs] = pv[0, e, zs] - scale * (pxp - pxm)
        u[1, e, zs] = pv[1, e, zs] - scale * (pz[2:] - pz[:-2])
        u[2, e, zs] = pv[2, e, zs] - scale * (next_y(p0, masks) - prev_y(p0, masks))

    even, low = lax.rem(lane, 2) == 0, lax.rem(lane, 4) < 2
    spread = jnp.where(lax.rem(lane, 4) == 0, fraction_spread, velocity_spread).astype(F32)

    def combine(a, b, by, mask):
        keep, other = jnp.where(mask, a, b), jnp.where(mask, b, a)
        return keep + jnp.where(mask, roll(other, LANE - by, 1), roll(other, by, 1))

    def restrict(c, out):
        def one(zc, _):
            sums = []
            for ref in (c, u.at[0], u.at[1], u.at[2]):
                total = None
                for i in range(ROWS):
                    part = ref[H + i, pl.ds(1 + 4 * zc, 4)]
                    total = part if total is None else total + part
                sums.append((total[0] + total[1]) + (total[2] + total[3]))
            pair = combine(sums[0], sums[1], 1, even), combine(sums[2], sums[3], 1, even)
            out[zc] = combine(pair[0], pair[1], 2, low) * (1.0 / 64.0)
            return 0
        lax.fori_loop(0, 4, one, 0)

    def diffuse(src, dst, length, out_reach):
        def one(j, _):
            v = src[j + 1]
            up = jnp.concatenate([v[1:], zero_line[None]], axis=0)
            down = jnp.concatenate([zero_line[None], v[:-1]], axis=0)
            around = src[j] + src[j + 2] + up + down + next_y(v, masks, by=4) + prev_y(v, masks, by=4)
            row = s + j - out_reach
            keep = ((row >= 0) & (row < SPACE)).astype(F32)
            dst[j] = (v + spread * (around - 6.0 * v)) * keep
            return 0
        lax.fori_loop(0, length, one, 0)

    def diffuse_down(src, reach, steps):
        now = src
        for step in range(steps):
            reach -= 1
            target = w0 if step % 2 == 0 else w1
            diffuse(now, target, 2 * reach + 1, reach)
            now = target
        return now

    first = row_copies([(c_a, 0, 2), (u.at[0], 0, 2), (u.at[1], 0, 1), (u.at[2], 0, 1)], 0)
    start(first)
    restrict(c_a, cstart.at[2])
    each_target(cstart.at[2], cstart, 2, 0, 0, "start")

    pending = [first]
    c, new_c = c_a, c_b
    for f in range(FINE):
        round_in = pending[-1]
        over((H + 1, H + ROWS - 1), lambda e, z0: advance(c, new_c, f, e, z0, 1, True))
        landed(round_in)
        over((H, H + 1), lambda e, z0: advance(c, new_c, f, e, z0, 1, True))
        over((H + ROWS - 1, H + ROWS), lambda e, z0: advance(c, new_c, f, e, z0, 1, True))
        fraction_rows = row_copies([(new_c, 1, 3)], 4 + 6 * f)
        start(fraction_rows)
        over((H - 1, H), lambda e, z0: advance(c, new_c, f, e, z0, 0, False))
        over((H + ROWS, H + ROWS + 1), lambda e, z0: advance(c, new_c, f, e, z0, 2, False))
        over((H, H + ROWS), lambda e, z0: first_pressure(new_c, e, z0))
        pressure_rows = row_copies([(p1, 0, 4)], 5 + 6 * f)
        start(pressure_rows)
        if f == 0:
            each_source(cstart.at[2], cstart, 2, 0, 0)
            done = diffuse_down(cstart, 2, 2)
            prev[...] = done[0] * (t > 0).astype(F32)
        landed(fraction_rows)
        over((1, H), lambda e, z0: face_block(new_c, e, z0, False))
        over((H + ROWS, EXT - 1), lambda e, z0: face_block(new_c, e, z0, False))
        over((H + 1, H + ROWS - 1), lambda e, z0: sweep(p1, p_a, e, z0))
        landed(pressure_rows)
        over((1, H + 1), lambda e, z0: sweep(p1, p_a, e, z0))
        over((H + ROWS - 1, EXT - 1), lambda e, z0: sweep(p1, p_a, e, z0))
        over((2, EXT - 2), lambda e, z0: sweep(p_a, p_b, e, z0))
        over((3, EXT - 3), lambda e, z0: sweep(p_b, p_a, e, z0))
        sent(round_in)
        over((H, H + ROWS), lambda e, z0: project(new_c, e, z0))
        sent(fraction_rows)
        sent(pressure_rows)
        if f == 0:
            again = row_copies([(u.at[0], 0, 2), (u.at[1], 0, 1), (u.at[2], 0, 1)], 6)
            start(again)
            pending.append(again)
        c, new_c = new_c, c
    each_target(cstart.at[2], cstart, 2, 0, 0, "sent")

    restrict(c, drive)
    drive[...] = drive[...] - prev[...]
    each_target(drive, rx1, 2, 1, 5, "start")
    each_target(drive, rx2, 4, 2, 10, "start")
    each_source(drive, rx2, 4, 2, 10)
    two = diffuse_down(rx2, 4, 2)
    each_source(drive, rx1, 2, 1, 5)

    def join(j, _):
        two[j] = two[j] + rx1[j]
        return 0
    lax.fori_loop(0, 5, join, 0)
    diffuse(two, w0, 3, 1)
    diffuse(w0, w1, 1, 0)
    t1[...] = w1[0]
    each_target(t1, rxs, 4, 2, 19, "start")
    each_source(t1, rxs, 4, 2, 19)
    t2[...] = t1[...] + diffuse_down(rxs, 4, 4)[0]
    each_target(t2, rxq, 8, 4, 28, "start")
    each_source(t2, rxq, 8, 4, 28)
    correction = (t2[...] + diffuse_down(rxq, 8, 8)[0]) - prev[...]
    w0[0] = correction

    stores = []
    for field in range(4):
        target = c if field == 0 else u.at[field - 1]

        def correct(zc, _, field=field, target=target):
            m = jnp.where(lax.rem(lane, 4) == field, w0[0, zc], 0.0)
            m = m + roll(m, 1 if field % 2 == 0 else LANE - 1, 1)
            m = m + roll(m, 2 if field < 2 else LANE - 2, 1)
            for i in range(ROWS):
                zs = pl.ds(1 + 4 * zc, 4)
                target[H + i, zs] = target[H + i, zs] + m[None]
            return 0
        lax.fori_loop(0, 4, correct, 0)
        for k in range(SUB):
            cols = pl.ds(LANE * k, LANE)
            home = ofrac_ref.at[0, :, :, cols] if field == 0 else ovel_ref.at[0, field - 1, :, :, cols]
            stores.append(pltpu.make_async_copy(
                target.at[pl.ds(H, ROWS), pl.ds(1, NZ), k, :], home, out_sem.at[field, k]))
            stores[-1].start()
    each_target(drive, rx1, 2, 1, 5, "sent")
    each_target(drive, rx2, 4, 2, 10, "sent")
    each_target(t1, rxs, 4, 2, 19, "sent")
    each_target(t2, rxq, 8, 4, 28, "sent")
    for c_ in stores:
        c_.wait()


def shards(fraction_levels, start_velocity, electrode_plan):
    line = (SUB, LANE)
    pad = (EXT, NZ + 2) + line
    flat = (EXT, NZ) + line
    row = (4,) + line

    def vmem(*shape):
        return pltpu.VMEM(shape, F32)

    return pl.pallas_call(
        kernel,
        out_shape=(
            jax.ShapeDtypeStruct(fraction_levels.shape, F32),
            jax.ShapeDtypeStruct(start_velocity.shape, F32),
        ),
        in_specs=[
            pl.BlockSpec(memory_space=pl.ANY),
            pl.BlockSpec(memory_space=pl.ANY),
            pl.BlockSpec(memory_space=pltpu.SMEM),
        ],
        out_specs=(pl.BlockSpec(memory_space=pl.ANY), pl.BlockSpec(memory_space=pl.ANY)),
        scratch_shapes=[
            pltpu.VMEM((ROWS, NZ) + line, jnp.int32),
            vmem(*pad), vmem(*pad),
            vmem(3, *pad), vmem(3, *pad),
            vmem(EXT + 1, NZ, *line), vmem(*pad), vmem(*flat), vmem(*flat), vmem(*flat),
            vmem(*pad), vmem(*pad), vmem(*pad),
            vmem(FINE, 3, *line), vmem(NZ, *line),
            vmem(5, *row), vmem(*row), vmem(*row),
            vmem(5, *row), vmem(9, *row), vmem(9, *row), vmem(17, *row),
            vmem(*row), vmem(*row), vmem(17, *row), vmem(17, *row),
            pltpu.SemaphoreType.DMA((4, SUB)), pltpu.SemaphoreType.DMA((4, SUB)),
            pltpu.SemaphoreType.DMA((12, 2)), pltpu.SemaphoreType.DMA((12, 2)),
            pltpu.SemaphoreType.DMA((45,)), pltpu.SemaphoreType.DMA((45,)),
        ],
        compiler_params=pltpu.CompilerParams(
            collective_id=0, has_side_effects=True, vmem_limit_bytes=48 * 2**20
        ),
    )(fraction_levels, start_velocity, electrode_plan)


def solution(mesh):
    return jax.shard_map(
        shards,
        mesh=mesh,
        in_specs=(
            P("tm", "space", None, None),
            P("tm", None, "space", None, None),
            P("tm", None, None),
        ),
        out_specs=(P("tm", "space", None, None), P("tm", None, "space", None, None)),
        check_vma=False,
    )
```

time: 552 us -> 107 us (0.19)
  starting transfers between devices: 308 us -> 0 us
  local copies, waits for them, and re-layouts: 132 us -> 4.35 us
  Pallas kernels: 0 us -> 101 us
  waiting for transfers between devices: 73.9 us -> 0 us
  other arithmetic: 30 us -> 0 us
    ppermute x71 -> x0, starting transfers between devices: 308 us -> none  [the longest x32 232 us: padded_2(): lax.ppermute(lax.slice_in_dim(block, block.shape[dim] - width, None, axis...]
    concatenate x8 -> x0, local copies, waits for them, and re-layouts: 116 us -> none  [the longest x4 58.8 us: fine_step(): stacked = jnp.concatenate([fraction[None], velocity])]
    pallas_call x0 -> x1, Pallas kernels: none -> 101 us  [shards(): pl.pallas_call(kernel, out_shape=(jax.ShapeDtypeStruct(fraction_levels.sh...]
    ppermute x71 -> x0, waiting for transfers between devices: 73.9 us -> none  [the longest x32 38.5 us: padded_2(): lax.ppermute(lax.slice_in_dim(block, block.shape[dim] - width, None, axis...]
    broadcast_in_dim x6 -> x0, local copies, waits for them, and re-layouts: 13.3 us -> none  [the longest x2 12.2 us: prolong(): jnp.broadcast_to(coarse[:, :, None, :, None, :, None], (parts, rows, 4, l...]
    mul x10 -> x0, other arithmetic: 7.92 us -> none  [the longest x8 7.21 us: relax_round(): current = current * inside[0:length, None, None]]
    add x29 -> x0, other arithmetic: 6.41 us -> none  [the longest x6 1.7 us: face_flux(): return jnp.maximum(speed, 0.0) * lower + jnp.minimum(speed, 0.0) * upper]
    concatenate x35 -> x0, other arithmetic: 6.33 us -> none  [the longest x32 6.21 us: padded_2(): block = jnp.concatenate([low, block, high], axis=dim)]
  transfers between devices with their start and end apart: 71 -> 0, of which waited for: 44 -> 0; matrix products, arithmetic and copies ran while one was open for 15% -> 0% of each run, Pallas kernels for 0% -> 0%
where the time goes in v1:
time: 107 us; the launch traced here: 106 us
  Pallas kernels  101 us (94%)
  local copies, waits for them, and re-layouts  4.35 us (4%)
    pallas_call x1, Pallas kernels, shards(): pl.pallas_call(kernel, out_shape=(jax.ShapeDtypeStruct(fraction_levels.sh...  101 us
    unnamed x8, local copies, waits for them, and re-layouts  4.35 us

profile of v1, /device:TPU:126, one launch (start us, length us, event | category | flops | bytes accessed | tf_op | source)
XLA Modules:
  0.0 105.6 jit_solution(1565824407173250978)
XLA Ops:
  0.6 0.0 copy-start
  0.6 1.1 %copy-done = f32[1,3,4,16,1024]{4,3,2,1,0:T(8,128)S(1)} copy-done((f32[1,3,4,16,1024]{4,3,2,1,0:T(8,128)S(1)}, f32[1,3,4,16,1024]{4,3,2,1,0:T(8,128)}, u32[]{:S(2)}) %copy-start) | copy-done | bytes 786456
  1.8 0.0 copy-start.1
  1.8 0.9 copy-done.1
  2.7 0.0 copy-start.2
  2.7 0.7 copy-done.2
  3.4 100.6 %shard_map.50 = (f32[1,4,16,1024]{3,2,1,0:T(8,128)S(1)}, f32[1,3,4,16,1024]{4,3,2,1,0:T(8,128)S(1)}) custom-call(s32[1,4,16,1024]{3,2,1,0:T(8,128)S(1)} %copy-done.1, f32[1,3,4,16,1024]{4,3,2,1,0:T(8,128)S(1)} %copy-done, s32[2,4,32]{2,1,0:T(4,128)S(1)} %copy-done.2), custom_call_target="tpu_custom_call" | custom-call | tf_op jit(solution)/shard_map/pallas_call | solution.py:505
  104.0 0.7 copy.7
  104.7 0.9 copy.8
Async XLA Ops:
  0.6 1.1 %copy-start = (f32[1,3,4,16,1024]{4,3,2,1,0:T(8,128)S(1)}, f32[1,3,4,16,1024]{4,3,2,1,0:T(8,128)}, u32[]{:S(2)}) copy-start(f32[1,3,4,16,1024]{4,3,2,1,0:T(8,128)} %vel_ref.1) | copy-start | bytes 2359300
  1.8 0.9 copy-start.1
  2.7 0.7 copy-start.2

commit v2 on v1

--- a/solution.py
+++ b/solution.py
@@ -19,7 +19,7 @@
 TILES = 4
 STRIPS = 32
 FINE = 2
-U = 4
+U = 16
 BLOCKS = NZ // U
 
 SLICES, SPACE = 8, 32
@@ -43,7 +43,8 @@
     ax = v.ndim
     r = roll(v, LANE - by, ax - 1)
     q = roll(r, SUB - 1, ax - 2)
-    q = jnp.where(masks["last_sub"], fill, q)
+    if fill is not None:
+        q = jnp.where(masks["last_sub"], fill, q)
     return jnp.where(masks["last_lane"] if by == 1 else masks["last_group"], q, r)
 
 
@@ -51,7 +52,8 @@
     ax = v.ndim
     r = roll(v, by, ax - 1)
     q = roll(r, 1, ax - 2)
-    q = jnp.where(masks["first_sub"], fill, q)
+    if fill is not None:
+        q = jnp.where(masks["first_sub"], fill, q)
     return jnp.where(masks["first_lane"] if by == 1 else masks["first_group"], q, r)
 
 
@@ -76,6 +78,7 @@
     masks = {
         "last_sub": sub == SUB - 1, "first_sub": sub == 0,
         "last_lane": lane == LANE - 1, "first_lane": lane == 0,
+        "last_cell": (sub == SUB - 1) & (lane == LANE - 1), "first_cell": (sub == 0) & (lane == 0),
         "last_group": lane >= LANE - 4, "first_group": lane < 4,
     }
 
@@ -160,12 +163,9 @@
     for k in range(SUB):
         loads[4 * k].wait()
 
-    def to_fraction(j, _):
-        i, z = lax.div(j, NZ), lax.rem(j, NZ)
-        c_a[H + i, 1 + z] = levb[i, z].astype(F32) * level_scale
-        return 0
-
-    lax.fori_loop(0, ROWS * NZ, to_fraction, 0)
+    for i in range(ROWS):
+        c_a[H + i, pl.ds(1, NZ)] = levb[i].astype(F32) * level_scale
+
     for k in range(SUB):
         for d in range(3):
             loads[4 * k + 1 + d].wait()
@@ -322,8 +322,8 @@
         gz[e, pl.ds(z0, U + 1)] = zface
         yl = 1.0 / (r0 + prev_y(r0, masks, 0.1))
         yu = 1.0 / (r0 + next_y(r0, masks, 0.1))
-        gyl[e, pl.ds(z0, U)] = yl
-        gyu[e, pl.ds(z0, U)] = yu
+        gyl[e, pl.ds(z0, U)] = jnp.where(masks["first_cell"], 0.0, yl)
+        gyu[e, pl.ds(z0, U)] = jnp.where(masks["last_cell"], 0.0, yu)
         total = lower + upper + (zface[:-1] + zface[1:]) + (yl + yu)
         inverse = 1.0 / total
         if not top:
@@ -345,7 +345,7 @@
         zface = gz[e, pl.ds(z0, U + 1)]
         summed = gx[e, pl.ds(z0, U)] * pxm + gx[e + 1, pl.ds(z0, U)] * pxp
         summed = summed + (zface[:-1] * pz[:-2] + zface[1:] * pz[2:])
-        summed = summed + (gyl[e, pl.ds(z0, U)] * prev_y(p0, masks) + gyu[e, pl.ds(z0, U)] * next_y(p0, masks))
+        summed = summed + (gyl[e, pl.ds(z0, U)] * prev_y(p0, masks, None) + gyu[e, pl.ds(z0, U)] * next_y(p0, masks, None))
         new[e, pl.ds(z0 + 1, U)] = p1[e, pl.ds(z0 + 1, U)] + rt[e, pl.ds(z0, U)] * summed
 
     def project(new_c, e, z0):
@@ -362,33 +362,31 @@
 
     def combine(a, b, by, mask):
         keep, other = jnp.where(mask, a, b), jnp.where(mask, b, a)
-        return keep + jnp.where(mask, roll(other, LANE - by, 1), roll(other, by, 1))
+        return keep + jnp.where(mask, roll(other, LANE - by, 2), roll(other, by, 2))
 
     def restrict(c, out):
-        def one(zc, _):
-            sums = []
-            for ref in (c, u.at[0], u.at[1], u.at[2]):
-                total = None
-                for i in range(ROWS):
-                    part = ref[H + i, pl.ds(1 + 4 * zc, 4)]
-                    total = part if total is None else total + part
-                sums.append((total[0] + total[1]) + (total[2] + total[3]))
-            pair = combine(sums[0], sums[1], 1, even), combine(sums[2], sums[3], 1, even)
-            out[zc] = combine(pair[0], pair[1], 2, low) * (1.0 / 64.0)
-            return 0
-        lax.fori_loop(0, 4, one, 0)
+        sums = []
+        for ref in (c, u.at[0], u.at[1], u.at[2]):
+            total = None
+            for i in range(ROWS):
+                part = ref[H + i, pl.ds(1, NZ)]
+                total = part if total is None else total + part
+            sums.append(jnp.sum(total.reshape(4, 4, SUB, LANE), axis=1))
+        pair = combine(sums[0], sums[1], 1, even), combine(sums[2], sums[3], 1, even)
+        out[...] = combine(pair[0], pair[1], 2, low) * (1.0 / 64.0)
 
     def diffuse(src, dst, length, out_reach):
-        def one(j, _):
-            v = src[j + 1]
-            up = jnp.concatenate([v[1:], zero_line[None]], axis=0)
-            down = jnp.concatenate([zero_line[None], v[:-1]], axis=0)
-            around = src[j] + src[j + 2] + up + down + next_y(v, masks, by=4) + prev_y(v, masks, by=4)
+        whole = src[pl.ds(0, length + 2)]
+        v = whole[1:-1]
+        edge = jnp.zeros((length, 1, SUB, LANE), F32)
+        up = jnp.concatenate([v[:, 1:], edge], axis=1)
+        down = jnp.concatenate([edge, v[:, :-1]], axis=1)
+        around = whole[:-2] + whole[2:] + up + down + next_y(v, masks, by=4) + prev_y(v, masks, by=4)
+        fresh = v + spread * (around - 6.0 * v)
+        for j in range(length):
             row = s + j - out_reach
             keep = ((row >= 0) & (row < SPACE)).astype(F32)
-            dst[j] = (v + spread * (around - 6.0 * v)) * keep
-            return 0
-        lax.fori_loop(0, length, one, 0)
+            dst[j] = fresh[j] * keep
 
     def diffuse_down(src, reach, steps):
         now = src
@@ -451,10 +449,7 @@
     two = diffuse_down(rx2, 4, 2)
     each_source(drive, rx1, 2, 1, 5)
 
-    def join(j, _):
-        two[j] = two[j] + rx1[j]
-        return 0
-    lax.fori_loop(0, 5, join, 0)
+    two[pl.ds(0, 5)] = two[pl.ds(0, 5)] + rx1[...]
     diffuse(two, w0, 3, 1)
     diffuse(w0, w1, 1, 0)
     t1[...] = w1[0]
@@ -464,21 +459,17 @@
     each_target(t2, rxq, 8, 4, 28, "start")
     each_source(t2, rxq, 8, 4, 28)
     correction = (t2[...] + diffuse_down(rxq, 8, 8)[0]) - prev[...]
-    w0[0] = correction
 
     stores = []
     for field in range(4):
         target = c if field == 0 else u.at[field - 1]
 
-        def correct(zc, _, field=field, target=target):
-            m = jnp.where(lax.rem(lane, 4) == field, w0[0, zc], 0.0)
-            m = m + roll(m, 1 if field % 2 == 0 else LANE - 1, 1)
-            m = m + roll(m, 2 if field < 2 else LANE - 2, 1)
-            for i in range(ROWS):
-                zs = pl.ds(1 + 4 * zc, 4)
-                target[H + i, zs] = target[H + i, zs] + m[None]
-            return 0
-        lax.fori_loop(0, 4, correct, 0)
+        m = jnp.where(lax.rem(lane, 4) == field, correction, 0.0)
+        m = m + roll(m, 1 if field % 2 == 0 else LANE - 1, 2)
+        m = m + roll(m, 2 if field < 2 else LANE - 2, 2)
+        m = jnp.broadcast_to(m[:, None], (4, 4, SUB, LANE)).reshape(NZ, SUB, LANE)
+        for i in range(ROWS):
+            target[H + i, pl.ds(1, NZ)] = target[H + i, pl.ds(1, NZ)] + m
         for k in range(SUB):
             cols = pl.ds(LANE * k, LANE)
             home = ofrac_ref.at[0, :, :, cols] if field == 0 else ovel_ref.at[0, field - 1, :, :, cols]
@@ -529,7 +520,7 @@
             pltpu.SemaphoreType.DMA((45,)), pltpu.SemaphoreType.DMA((45,)),
         ],
         compiler_params=pltpu.CompilerParams(
-            collective_id=0, has_side_effects=True, vmem_limit_bytes=48 * 2**20
+            collective_id=0, has_side_effects=True, vmem_limit_bytes=62 * 2**20
         ),
     )(fraction_levels, start_velocity, electrode_plan)
 

time: 107 us -> 85 us (0.79)
  Pallas kernels: 101 us -> 79.6 us
    pallas_call x1, Pallas kernels: 101 us -> 79.6 us  [shards(): pl.pallas_call(kernel, out_shape=(jax.ShapeDtypeStruct(fraction_levels.sh...]
    unnamed x8 -> x2, local copies, waits for them, and re-layouts: 4.35 us -> 3.76 us
where the time goes in v2:
time: 85 us; the launch traced here: 84 us
  Pallas kernels  79.6 us (94%)
  local copies, waits for them, and re-layouts  3.76 us (4%)
    pallas_call x1, Pallas kernels, shards(): pl.pallas_call(kernel, out_shape=(jax.ShapeDtypeStruct(fraction_levels.sh...  79.6 us
    unnamed x2, local copies, waits for them, and re-layouts  3.76 us

profile of v2, /device:TPU:126, one launch (start us, length us, event | category | flops | bytes accessed | tf_op | source)
XLA Modules:
  0.0 84.0 jit_solution(9529425332034925845)
XLA Ops:
  0.6 79.6 %shard_map.50 = (f32[1,4,16,1024]{3,2,1,0:T(8,128)}, f32[1,3,4,16,1024]{4,3,2,1,0:T(8,128)}) custom-call(s32[1,4,16,1024]{3,2,1,0:T(8,128)} %lev_ref.1, f32[1,3,4,16,1024]{4,3,2,1,0:T(8,128)} %vel_ref.1, s32[2,4,32]{2,1,0:T(4,128)} %plan_ref.1), custom_call_target="tpu_custom_call" | custom-call | tf_op jit(solution)/shard_map/pallas_call | solution.py:496
  80.3 1.7 %copy.7 = f32[1,4,16,1024]{3,2,1,0:T(8,128)} copy(f32[1,4,16,1024]{3,2,1,0:T(8,128)} %get-tuple-element.4) | data formatting | bytes 524288
  81.9 2.1 %copy.8 = f32[1,3,4,16,1024]{4,3,2,1,0:T(8,128)} copy(f32[1,3,4,16,1024]{4,3,2,1,0:T(8,128)} %get-tuple-element.5) | data formatting | bytes 1572864

commit v3 on v2

--- a/solution.py
+++ b/solution.py
@@ -69,8 +69,8 @@
 def kernel(
     lev_ref, vel_ref, plan_ref, ofrac_ref, ovel_ref,
     levb, c_a, c_b, u, pv, gx, gz, gyl, gyu, rt, p1, p_a, p_b, elec, wall,
-    cstart, prev, drive, rx1, rx2, rxs, rxq, t1, t2, w0, w1,
-    in_sem, out_sem, fs_send, fs_recv, cs_send, cs_recv,
+    cstart, prev, drive, rx1, rx2, rx3, rxs, rxq, part, w0, w1,
+    in_sem, out_sem, fs_send, fs_recv, cs_send, cs_recv, hand_sem,
 ):
     t = lax.axis_index("tm")
     s = lax.axis_index("space")
@@ -98,6 +98,27 @@
         c.start()
 
     zero_line = jnp.zeros((SUB, LANE), F32)
+    cstart[...] = jnp.zeros(cstart.shape, F32)
+
+    barrier = pltpu.get_barrier_semaphore()
+    beside = [(0, 1), (0, -1), (1, 0), (-1, 0)]
+
+    def tell(semaphore, places):
+        for dt, ds in places:
+            @pl.when(there(dt, ds))
+            def _(dt=dt, ds=ds):
+                pl.semaphore_signal(semaphore, inc=1, device_id=(t + dt, s + ds), device_id_type=MESH)
+
+    def hear(semaphore, places):
+        count = jnp.int32(0)
+        for dt, ds in places:
+            count = count + there(dt, ds).astype(jnp.int32)
+
+        @pl.when(count > 0)
+        def _():
+            pl.semaphore_wait(semaphore, count)
+
+    tell(barrier, beside)
 
     def zero_pads(e, _):
         for ref in (c_a, c_b, p1, p_a, p_b, pv.at[1], u.at[0], u.at[1], u.at[2]):
@@ -105,64 +126,42 @@
             ref[e, NZ + 1] = zero_line
         return 0
 
-    lax.fori_loop(0, EXT, zero_pads, 0)
-
     def zero_rows(first):
-        def one(j, _):
-            z = 1 + lax.rem(j, NZ)
-            e = first + lax.div(j, NZ)
+        def one(e, _):
             for ref in (c_a, c_b, p1, u.at[0], u.at[1], u.at[2]):
-                ref[e, z] = zero_line
+                ref[e] = jnp.zeros((NZ + 2, SUB, LANE), F32)
             return 0
-        lax.fori_loop(0, H * NZ, one, 0)
-
-    @pl.when(s == 0)
-    def _():
-        zero_rows(0)
-
-    @pl.when(s == SPACE - 1)
-    def _():
-        zero_rows(H + ROWS)
-
-    zero_coarse = jnp.zeros((4, SUB, LANE), F32)
-    for ref in (cstart, rx1, rx2, rxs, rxq):
-        def one_row(j, _, ref=ref):
-            ref[j] = zero_coarse
-            return 0
-        lax.fori_loop(0, ref.shape[0], one_row, 0)
-
-    barrier = pltpu.get_barrier_semaphore()
-    groups = [(0, 2)] + [(sign * k, r) for k, r in ((1, 2), (2, 4), (4, 8)) for sign in (1, -1)]
-    expected = jnp.int32(0)
-    for dt, reach in groups:
-        def greet(j, count, dt=dt, reach=reach):
-            ds = j - reach
-            ok = there(dt, ds)
-            if dt == 0:
-                ok = ok & (ds != 0)
-
-            @pl.when(ok)
-            def _():
-                pl.semaphore_signal(barrier, inc=1, device_id=(t + dt, s + ds), device_id_type=MESH)
-
-            return count + ok.astype(jnp.int32)
-        expected = lax.fori_loop(0, 2 * reach + 1, greet, expected)
-
-    strip = sub * 4 + lax.div(lane, TILE)
+        lax.fori_loop(first, first + H, one, 0)
+
+    def fill_tables():
+        lax.fori_loop(0, EXT, zero_pads, 0)
+
+        @pl.when(s == 0)
+        def _():
+            zero_rows(0)
+
+        @pl.when(s == SPACE - 1)
+        def _():
+            zero_rows(H + ROWS)
+
+        for ref in (rx1, rx2, rx3, rxs, rxq):
+            ref[...] = jnp.zeros(ref.shape, F32)
+        strip = sub * 4 + lax.div(lane, TILE)
+        tiles = [jnp.clip(lax.div(first_row - 1 + TILE, TILE) - 1, 0, TILES - 1), lax.div(first_row, TILE),
+                 jnp.clip(lax.div(first_row + ROWS, TILE), 0, TILES - 1)]
+        for f in range(FINE):
+            def paint(q, fields, f=f):
+                return tuple(jnp.where(strip == q, plan_ref[f, tile, q].astype(F32), field)
+                             for tile, field in zip(tiles, fields))
+            painted = lax.fori_loop(0, STRIPS, paint, (zero_line,) * 3, unroll=4)
+            for j in range(3):
+                elec[f, j] = painted[j]
+        for z in range(NZ):
+            wall[z] = jnp.full((SUB, LANE), wall_scale, F32) * jnp.exp(jnp.full((SUB, LANE), -z / wall_decay, F32))
+
     first_row = s * ROWS
-    tiles = [jnp.clip(lax.div(first_row - 1 + TILE, TILE) - 1, 0, TILES - 1), lax.div(first_row, TILE),
-             jnp.clip(lax.div(first_row + ROWS, TILE), 0, TILES - 1)]
-    for f in range(FINE):
-        for j, tile in enumerate(tiles):
-            def paint(q, field, f=f, tile=tile):
-                return jnp.where(strip == q, plan_ref[f, tile, q].astype(F32), field)
-            elec[f, j] = lax.fori_loop(0, STRIPS, paint, zero_line)
-    for z in range(NZ):
-        wall[z] = jnp.full((SUB, LANE), wall_scale, F32) * jnp.exp(jnp.full((SUB, LANE), -z / wall_decay, F32))
-
     for k in range(SUB):
         loads[4 * k].wait()
-
     for i in range(ROWS):
         c_a[H + i, pl.ds(1, NZ)] = levb[i].astype(F32) * level_scale
 
@@ -170,7 +169,7 @@
         for d in range(3):
             loads[4 * k + 1 + d].wait()
 
-    pl.semaphore_wait(barrier, expected)
+    hear(barrier, beside)
 
     def row_copies(entries, base):
         rights, lefts = [], []
@@ -228,40 +227,56 @@
             for c in lefts:
                 c.wait_send()
 
-    def coarse_copy(src, dst, reach, dt, base, ds):
+    def coarse_copy(link, src, ds):
+        dst, reach, dt, base, lo, hi = link
         j = reach - ds
         return pltpu.make_async_remote_copy(
             src_ref=src, dst_ref=dst.at[j], send_sem=cs_send.at[base + j], recv_sem=cs_recv.at[base + j],
             device_id=(t + dt, s + ds), device_id_type=MESH)
 
-    def each_target(src, dst, reach, dt, base, action):
-        def one(j, _):
-            ds = j - reach
-            ok = there(dt, ds)
-            if dt == 0:
-                ok = ok & (ds != 0)
-
-            @pl.when(ok)
-            def _():
-                c = coarse_copy(src, dst, reach, dt, base, ds)
-                c.start() if action == "start" else c.wait_send()
-
-            return 0
-        lax.fori_loop(0, 2 * reach + 1, one, 0)
-
-    def each_source(src, dst, reach, dt, base):
-        def one(j, _):
-            ds = reach - j
-            ok = there(-dt, -ds)
-            if dt == 0:
-                ok = ok & (ds != 0)
-
-            @pl.when(ok)
-            def _():
-                coarse_copy(src, dst, reach, dt, base, ds).wait_recv()
-
-            return 0
-        lax.fori_loop(0, 2 * reach + 1, one, 0)
+    def each_target(link, src, action):
+        dst, reach, dt, base, lo, hi = link
+
+        @pl.when((t >= lo) & (t <= hi))
+        def _():
+            def one(j, _):
+                ds = j - reach
+                ok = there(dt, ds)
+                if dt == 0:
+                    ok = ok & (ds != 0)
+
+                @pl.when(ok)
+                def _():
+                    c = coarse_copy(link, src, ds)
+                    c.start() if action == "start" else c.wait_send()
+
+                return 0
+            lax.fori_loop(0, 2 * reach + 1, one, 0)
+
+    def each_source(link, src):
+        dst, reach, dt, base, lo, hi = link
+
+        @pl.when((t - dt >= lo) & (t - dt <= hi))
+        def _():
+            def one(j, _):
+                ds = reach - j
+                ok = there(-dt, -ds)
+                if dt == 0:
+                    ok = ok & (ds != 0)
+
+                @pl.when(ok)
+                def _():
+                    coarse_copy(link, src, ds).wait_recv()
+
+                return 0
+            lax.fori_loop(0, 2 * reach + 1, one, 0)
+
+    starts = (cstart, 2, 0, 0, 0, SLICES - 1)
+    one_back = (rx1, 2, 1, 5, 0, SLICES - 2)
+    two_back = (rx2, 4, 2, 10, 0, SLICES - 3)
+    three_back = (rx3, 6, 3, 19, 0, 0)
+    sum_two = (rxs, 4, 2, 32, 2, 5)
+    sum_four = (rxq, 8, 4, 41, 2, 3)
 
     def inside(row):
         return ((row >= 0) & (row < SPACE * ROWS)).astype(F32)
@@ -399,8 +414,9 @@
 
     first = row_copies([(c_a, 0, 2), (u.at[0], 0, 2), (u.at[1], 0, 1), (u.at[2], 0, 1)], 0)
     start(first)
+    tell(hand_sem.at[0], [(1, 0), (-1, 0)])
+    fill_tables()
     restrict(c_a, cstart.at[2])
-    each_target(cstart.at[2], cstart, 2, 0, 0, "start")
 
     pending = [first]
     c, new_c = c_a, c_b
@@ -408,6 +424,13 @@
         round_in = pending[-1]
         over((H + 1, H + ROWS - 1), lambda e, z0: advance(c, new_c, f, e, z0, 1, True))
         landed(round_in)
+        if f == 0:
+            each_target(starts, cstart.at[2], "start")
+            hear(hand_sem.at[0], [(1, 0), (-1, 0)])
+            tell(hand_sem.at[1], [(2, 0), (-2, 0)])
+        else:
+            hear(hand_sem.at[1], [(2, 0), (-2, 0)])
+            tell(hand_sem.at[2], [(0, 4), (0, -4)])
         over((H, H + 1), lambda e, z0: advance(c, new_c, f, e, z0, 1, True))
         over((H + ROWS - 1, H + ROWS), lambda e, z0: advance(c, new_c, f, e, z0, 1, True))
         fraction_rows = row_copies([(new_c, 1, 3)], 4 + 6 * f)
@@ -418,10 +441,13 @@
         pressure_rows = row_copies([(p1, 0, 4)], 5 + 6 * f)
         start(pressure_rows)
         if f == 0:
-            each_source(cstart.at[2], cstart, 2, 0, 0)
+            each_source(starts, cstart.at[2])
             done = diffuse_down(cstart, 2, 2)
             prev[...] = done[0] * (t > 0).astype(F32)
         landed(fraction_rows)
+        if f == 1:
+            hear(hand_sem.at[2], [(0, 4), (0, -4)])
+            tell(hand_sem.at[3], [(-k, 0) for k in (1, 2, 3, 4)])
         over((1, H), lambda e, z0: face_block(new_c, e, z0, False))
         over((H + ROWS, EXT - 1), lambda e, z0: face_block(new_c, e, z0, False))
         over((H + 1, H + ROWS - 1), lambda e, z0: sweep(p1, p_a, e, z0))
@@ -439,26 +465,33 @@
             start(again)
             pending.append(again)
         c, new_c = new_c, c
-    each_target(cstart.at[2], cstart, 2, 0, 0, "sent")
+    each_target(starts, cstart.at[2], "sent")
 
     restrict(c, drive)
     drive[...] = drive[...] - prev[...]
-    each_target(drive, rx1, 2, 1, 5, "start")
-    each_target(drive, rx2, 4, 2, 10, "start")
-    each_source(drive, rx2, 4, 2, 10)
-    two = diffuse_down(rx2, 4, 2)
-    each_source(drive, rx1, 2, 1, 5)
-
-    two[pl.ds(0, 5)] = two[pl.ds(0, 5)] + rx1[...]
-    diffuse(two, w0, 3, 1)
+    hear(hand_sem.at[3], [(k, 0) for k in (1, 2, 3, 4)])
+    each_target(three_back, drive, "start")
+    each_target(two_back, drive, "start")
+    each_target(one_back, drive, "start")
+    each_source(three_back, drive)
+    three = diffuse_down(rx3, 6, 2)
+    each_source(two_back, drive)
+    three[pl.ds(0, 9)] = three[pl.ds(0, 9)] + rx2[...]
+    diffuse(three, w0, 7, 3)
+    diffuse(w0, w1, 5, 2)
+    each_source(one_back, drive)
+    w1[pl.ds(0, 5)] = w1[pl.ds(0, 5)] + rx1[...]
+    diffuse(w1, w0, 3, 1)
     diffuse(w0, w1, 1, 0)
-    t1[...] = w1[0]
-    each_target(t1, rxs, 4, 2, 19, "start")
-    each_source(t1, rxs, 4, 2, 19)
-    t2[...] = t1[...] + diffuse_down(rxs, 4, 4)[0]
-    each_target(t2, rxq, 8, 4, 28, "start")
-    each_source(t2, rxq, 8, 4, 28)
-    correction = (t2[...] + diffuse_down(rxq, 8, 8)[0]) - prev[...]
+    part[...] = w1[0]
+    each_target(sum_four, part, "start")
+    each_target(sum_two, part, "start")
+    each_source(sum_four, part)
+    eight = diffuse_down(rxq, 8, 4)
+    each_source(sum_two, part)
+    eight[pl.ds(0, 9)] = eight[pl.ds(0, 9)] + rxs[...]
+    four = diffuse_down(eight, 4, 4)
+    correction = (part[...] + four[0]) - prev[...]
 
     stores = []
     for field in range(4):
@@ -476,10 +509,11 @@
             stores.append(pltpu.make_async_copy(
                 target.at[pl.ds(H, ROWS), pl.ds(1, NZ), k, :], home, out_sem.at[field, k]))
             stores[-1].start()
-    each_target(drive, rx1, 2, 1, 5, "sent")
-    each_target(drive, rx2, 4, 2, 10, "sent")
-    each_target(t1, rxs, 4, 2, 19, "sent")
-    each_target(t2, rxq, 8, 4, 28, "sent")
+    each_target(three_back, drive, "sent")
+    each_target(two_back, drive, "sent")
+    each_target(one_back, drive, "sent")
+    each_target(sum_four, part, "sent")
+    each_target(sum_two, part, "sent")
     for c_ in stores:
         c_.wait()
 
@@ -513,11 +547,12 @@
             vmem(*pad), vmem(*pad), vmem(*pad),
             vmem(FINE, 3, *line), vmem(NZ, *line),
             vmem(5, *row), vmem(*row), vmem(*row),
-            vmem(5, *row), vmem(9, *row), vmem(9, *row), vmem(17, *row),
-            vmem(*row), vmem(*row), vmem(17, *row), vmem(17, *row),
+            vmem(5, *row), vmem(9, *row), vmem(13, *row), vmem(9, *row), vmem(17, *row),
+            vmem(*row), vmem(17, *row), vmem(17, *row),
             pltpu.SemaphoreType.DMA((4, SUB)), pltpu.SemaphoreType.DMA((4, SUB)),
             pltpu.SemaphoreType.DMA((12, 2)), pltpu.SemaphoreType.DMA((12, 2)),
-            pltpu.SemaphoreType.DMA((45,)), pltpu.SemaphoreType.DMA((45,)),
+            pltpu.SemaphoreType.DMA((58,)), pltpu.SemaphoreType.DMA((58,)),
+            pltpu.SemaphoreType.REGULAR((4,)),
         ],
         compiler_params=pltpu.CompilerParams(
             collective_id=0, has_side_effects=True, vmem_limit_bytes=62 * 2**20

time: 85 us -> 79.2 us (0.932)
  Pallas kernels: 79.6 us -> 74.5 us
    pallas_call x1, Pallas kernels: 79.6 us -> 74.5 us  [shards(): pl.pallas_call(kernel, out_shape=(jax.ShapeDtypeStruct(fraction_levels.sh...]
where the time goes in v3:
time: 79.2 us; the launch traced here: 78.9 us
  Pallas kernels  74.5 us (94%)
  local copies, waits for them, and re-layouts  3.76 us (5%)
    pallas_call x1, Pallas kernels, shards(): pl.pallas_call(kernel, out_shape=(jax.ShapeDtypeStruct(fraction_levels.sh...  74.5 us
    unnamed x2, local copies, waits for them, and re-layouts  3.76 us

profile of v3, /device:TPU:126, one launch (start us, length us, event | category | flops | bytes accessed | tf_op | source)
XLA Modules:
  0.0 78.9 jit_solution(4121279394707815694)
XLA Ops:
  0.6 74.5 %shard_map.50 = (f32[1,4,16,1024]{3,2,1,0:T(8,128)}, f32[1,3,4,16,1024]{4,3,2,1,0:T(8,128)}) custom-call(s32[1,4,16,1024]{3,2,1,0:T(8,128)} %lev_ref.1, f32[1,3,4,16,1024]{4,3,2,1,0:T(8,128)} %vel_ref.1, s32[2,4,32]{2,1,0:T(4,128)} %plan_ref.1), custom_call_target="tpu_custom_call" | custom-call | tf_op jit(solution)/shard_map/pallas_call | solution.py:530
  75.2 1.7 %copy.7 = f32[1,4,16,1024]{3,2,1,0:T(8,128)} copy(f32[1,4,16,1024]{3,2,1,0:T(8,128)} %get-tuple-element.4) | data formatting | bytes 524288
  76.9 2.1 %copy.8 = f32[1,3,4,16,1024]{4,3,2,1,0:T(8,128)} copy(f32[1,3,4,16,1024]{4,3,2,1,0:T(8,128)} %get-tuple-element.5) | data formatting | bytes 1572864

commit v4 on v3

--- a/solution.py
+++ b/solution.py
@@ -412,58 +412,99 @@
             now = target
         return now
 
-    first = row_copies([(c_a, 0, 2), (u.at[0], 0, 2), (u.at[1], 0, 1), (u.at[2], 0, 1)], 0)
-    start(first)
+    near = row_copies([(c_a, 0, 1), (u.at[0], 0, 1), (u.at[1], 0, 1), (u.at[2], 0, 1)], 0)
+    far = row_copies([(c_a, 1, 1), (u.at[0], 1, 1)], 4)
+    start(near)
+    start(far)
     tell(hand_sem.at[0], [(1, 0), (-1, 0)])
     fill_tables()
     restrict(c_a, cstart.at[2])
 
-    pending = [first]
+    def both(body, *rows):
+        for e in rows:
+            body(e, 0)
+
     c, new_c = c_a, c_b
+    last = H + ROWS - 1
     for f in range(FINE):
-        round_in = pending[-1]
-        over((H + 1, H + ROWS - 1), lambda e, z0: advance(c, new_c, f, e, z0, 1, True))
-        landed(round_in)
+        def step_full(e, z0):
+            advance(c, new_c, f, e, z0, 1, True)
+
+        def faces(e, z0):
+            face_block(new_c, e, z0, False)
+
+        def first_p(e, z0):
+            first_pressure(new_c, e, z0)
+
+        def sweep_1(e, z0):
+            sweep(p1, p_a, e, z0)
+
+        def sweep_2(e, z0):
+            sweep(p_a, p_b, e, z0)
+
+        def sweep_3(e, z0):
+            sweep(p_b, p_a, e, z0)
+
+        base = 6 + 10 * f
+        over((H + 1, last), step_full)
+        fraction_mid = row_copies([(new_c, 1, 2)], base)
+        start(fraction_mid)
+        landed(near)
+        both(step_full, H, last)
+        fraction_far = row_copies([(new_c, 3, 1)], base + 1)
+        start(fraction_far)
+        over((H + 1, last), first_p)
+        pressure_mid = row_copies([(p1, 1, 2)], base + 2)
+        start(pressure_mid)
         if f == 0:
-            each_target(starts, cstart.at[2], "start")
             hear(hand_sem.at[0], [(1, 0), (-1, 0)])
             tell(hand_sem.at[1], [(2, 0), (-2, 0)])
+            each_target(starts, cstart.at[2], "start")
         else:
             hear(hand_sem.at[1], [(2, 0), (-2, 0)])
             tell(hand_sem.at[2], [(0, 4), (0, -4)])
-        over((H, H + 1), lambda e, z0: advance(c, new_c, f, e, z0, 1, True))
-        over((H + ROWS - 1, H + ROWS), lambda e, z0: advance(c, new_c, f, e, z0, 1, True))
-        fraction_rows = row_copies([(new_c, 1, 3)], 4 + 6 * f)
-        start(fraction_rows)
-        over((H - 1, H), lambda e, z0: advance(c, new_c, f, e, z0, 0, False))
-        over((H + ROWS, H + ROWS + 1), lambda e, z0: advance(c, new_c, f, e, z0, 2, False))
-        over((H, H + ROWS), lambda e, z0: first_pressure(new_c, e, z0))
-        pressure_rows = row_copies([(p1, 0, 4)], 5 + 6 * f)
-        start(pressure_rows)
+        landed(far)
+        advance(c, new_c, f, H - 1, 0, 0, False)
+        advance(c, new_c, f, last + 1, 0, 2, False)
+        both(first_p, H, last)
+        pressure_near = row_copies([(p1, 0, 1)], base + 3)
+        pressure_far = row_copies([(p1, 3, 1)], base + 4)
+        start(pressure_near)
+        start(pressure_far)
+        over((H + 1, last), sweep_1)
+        landed(fraction_mid)
+        both(faces, H - 1, last + 1)
+        landed(fraction_far)
+        both(faces, H - 2, last + 2)
+        both(faces, H - 3, last + 3)
         if f == 0:
             each_source(starts, cstart.at[2])
             done = diffuse_down(cstart, 2, 2)
             prev[...] = done[0] * (t > 0).astype(F32)
-        landed(fraction_rows)
-        if f == 1:
+        else:
             hear(hand_sem.at[2], [(0, 4), (0, -4)])
             tell(hand_sem.at[3], [(-k, 0) for k in (1, 2, 3, 4)])
-        over((1, H), lambda e, z0: face_block(new_c, e, z0, False))
-        over((H + ROWS, EXT - 1), lambda e, z0: face_block(new_c, e, z0, False))
-        over((H + 1, H + ROWS - 1), lambda e, z0: sweep(p1, p_a, e, z0))
-        landed(pressure_rows)
-        over((1, H + 1), lambda e, z0: sweep(p1, p_a, e, z0))
-        over((H + ROWS - 1, EXT - 1), lambda e, z0: sweep(p1, p_a, e, z0))
-        over((2, EXT - 2), lambda e, z0: sweep(p_a, p_b, e, z0))
-        over((3, EXT - 3), lambda e, z0: sweep(p_b, p_a, e, z0))
-        sent(round_in)
+        landed(pressure_mid)
+        landed(pressure_near)
+        both(sweep_1, H, last)
+        both(sweep_1, H - 1, last + 1)
+        both(sweep_1, H - 2, last + 2)
+        over((H - 1, last + 2), sweep_2)
+        over((H, last + 1), sweep_3)
+        landed(pressure_far)
+        both(sweep_1, H - 3, last + 3)
+        both(sweep_2, H - 2, last + 2)
+        both(sweep_3, H - 1, last + 1)
+        sent(near)
+        sent(far)
         over((H, H + ROWS), lambda e, z0: project(new_c, e, z0))
-        sent(fraction_rows)
-        sent(pressure_rows)
         if f == 0:
-            again = row_copies([(u.at[0], 0, 2), (u.at[1], 0, 1), (u.at[2], 0, 1)], 6)
-            start(again)
-            pending.append(again)
+            near = row_copies([(u.at[0], 0, 1), (u.at[1], 0, 1), (u.at[2], 0, 1)], 26)
+            far = row_copies([(u.at[0], 1, 1)], 29)
+            start(near)
+            start(far)
+        for copies in (fraction_mid, fraction_far, pressure_mid, pressure_near, pressure_far):
+            sent(copies)
         c, new_c = new_c, c
     each_target(starts, cstart.at[2], "sent")
 
@@ -550,7 +591,7 @@
             vmem(5, *row), vmem(9, *row), vmem(13, *row), vmem(9, *row), vmem(17, *row),
             vmem(*row), vmem(17, *row), vmem(17, *row),
             pltpu.SemaphoreType.DMA((4, SUB)), pltpu.SemaphoreType.DMA((4, SUB)),
-            pltpu.SemaphoreType.DMA((12, 2)), pltpu.SemaphoreType.DMA((12, 2)),
+            pltpu.SemaphoreType.DMA((30, 2)), pltpu.SemaphoreType.DMA((30, 2)),
             pltpu.SemaphoreType.DMA((58,)), pltpu.SemaphoreType.DMA((58,)),
             pltpu.SemaphoreType.REGULAR((4,)),
         ],

time: 79.2 us -> 72.7 us (0.918)
  Pallas kernels: 74.5 us -> 68 us
    pallas_call x1, Pallas kernels: 74.5 us -> 68 us  [shards(): pl.pallas_call(kernel, out_shape=(jax.ShapeDtypeStruct(fraction_levels.sh...]
where the time goes in v4:
time: 72.7 us; the launch traced here: 72.4 us
  Pallas kernels  68 us (94%)
  local copies, waits for them, and re-layouts  3.76 us (5%)
    pallas_call x1, Pallas kernels, shards(): pl.pallas_call(kernel, out_shape=(jax.ShapeDtypeStruct(fraction_levels.sh...  68 us
    unnamed x2, local copies, waits for them, and re-layouts  3.76 us

profile of v4, /device:TPU:126, one launch (start us, length us, event | category | flops | bytes accessed | tf_op | source)
XLA Modules:
  0.0 72.4 jit_solution(622459702717736901)
XLA Ops:
  0.6 68.0 %shard_map.50 = (f32[1,4,16,1024]{3,2,1,0:T(8,128)}, f32[1,3,4,16,1024]{4,3,2,1,0:T(8,128)}) custom-call(s32[1,4,16,1024]{3,2,1,0:T(8,128)} %lev_ref.1, f32[1,3,4,16,1024]{4,3,2,1,0:T(8,128)} %vel_ref.1, s32[2,4,32]{2,1,0:T(4,128)} %plan_ref.1), custom_call_target="tpu_custom_call" | custom-call | tf_op jit(solution)/shard_map/pallas_call | solution.py:571
  68.6 1.7 %copy.7 = f32[1,4,16,1024]{3,2,1,0:T(8,128)} copy(f32[1,4,16,1024]{3,2,1,0:T(8,128)} %get-tuple-element.4) | data formatting | bytes 524288
  70.3 2.1 %copy.8 = f32[1,3,4,16,1024]{4,3,2,1,0:T(8,128)} copy(f32[1,3,4,16,1024]{4,3,2,1,0:T(8,128)} %get-tuple-element.5) | data formatting | bytes 1572864

commit v5 on v4

--- a/solution.py
+++ b/solution.py
@@ -67,9 +67,9 @@
 
 
 def kernel(
-    lev_ref, vel_ref, plan_ref, ofrac_ref, ovel_ref,
+    lev_ref, vel_ref, plan_ref, ofrac_ref, ovel_ref, cfrac_ref, cvel_ref,
     levb, c_a, c_b, u, pv, gx, gz, gyl, gyu, rt, p1, p_a, p_b, elec, wall,
-    cstart, prev, drive, rx1, rx2, rx3, rxs, rxq, part, w0, w1,
+    cstart, prev, drive, rx1, rx2, rx3, rxs, rxq, part, w0, w1, wide,
     in_sem, out_sem, fs_send, fs_recv, cs_send, cs_recv, hand_sem,
 ):
     t = lax.axis_index("tm")
@@ -87,15 +87,17 @@
 
     has_left, has_right = s > 0, s < SPACE - 1
 
-    loads = []
-    for k in range(SUB):
-        cols = pl.ds(LANE * k, LANE)
-        loads.append(pltpu.make_async_copy(lev_ref.at[0, :, :, cols], levb.at[:, :, k, :], in_sem.at[0, k]))
-        for d in range(3):
-            loads.append(pltpu.make_async_copy(
-                vel_ref.at[0, d, :, :, cols], u.at[d, pl.ds(H, ROWS), pl.ds(1, NZ), k, :], in_sem.at[1 + d, k]))
-    for c in loads:
-        c.start()
+    loads = {}
+    for i in (0, ROWS - 1, 1, 2):
+        loads[i] = []
+        for k in range(SUB):
+            cols = pl.ds(LANE * k, LANE)
+            loads[i].append(pltpu.make_async_copy(
+                lev_ref.at[0, i, :, cols], levb.at[i, :, k, :], in_sem.at[0, i, k]))
+            loads[i].append(pltpu.make_async_copy(
+                vel_ref.at[0, :, i, :, cols], u.at[:, H + i, pl.ds(1, NZ), k, :], in_sem.at[1, i, k]))
+        for n, c in enumerate(loads[i]):
+            c.start(priority=n // 2 % 2)
 
     zero_line = jnp.zeros((SUB, LANE), F32)
     cstart[...] = jnp.zeros(cstart.shape, F32)
@@ -160,15 +162,13 @@
             wall[z] = jnp.full((SUB, LANE), wall_scale, F32) * jnp.exp(jnp.full((SUB, LANE), -z / wall_decay, F32))
 
     first_row = s * ROWS
-    for k in range(SUB):
-        loads[4 * k].wait()
-    for i in range(ROWS):
+    def load(i):
+        for c in loads[i]:
+            c.wait()
         c_a[H + i, pl.ds(1, NZ)] = levb[i].astype(F32) * level_scale
 
-    for k in range(SUB):
-        for d in range(3):
-            loads[4 * k + 1 + d].wait()
-
+    load(0)
+    load(ROWS - 1)
     hear(barrier, beside)
 
     def row_copies(entries, base):
@@ -415,6 +415,8 @@
     near = row_copies([(c_a, 0, 1), (u.at[0], 0, 1), (u.at[1], 0, 1), (u.at[2], 0, 1)], 0)
     far = row_copies([(c_a, 1, 1), (u.at[0], 1, 1)], 4)
     start(near)
+    load(1)
+    load(2)
     start(far)
     tell(hand_sem.at[0], [(1, 0), (-1, 0)])
     fill_tables()
@@ -508,12 +510,21 @@
         c, new_c = new_c, c
     each_target(starts, cstart.at[2], "sent")
 
+    stores = []
+    for k in range(SUB):
+        cols = pl.ds(LANE * k, LANE)
+        stores.append(pltpu.make_async_copy(
+            c.at[pl.ds(H, ROWS), pl.ds(1, NZ), k, :], ofrac_ref.at[0, :, :, cols], out_sem.at[0, k]))
+        stores.append(pltpu.make_async_copy(
+            u.at[:, pl.ds(H, ROWS), pl.ds(1, NZ), k, :], ovel_ref.at[0, :, :, :, cols], out_sem.at[1, k]))
     restrict(c, drive)
     drive[...] = drive[...] - prev[...]
     hear(hand_sem.at[3], [(k, 0) for k in (1, 2, 3, 4)])
     each_target(three_back, drive, "start")
     each_target(two_back, drive, "start")
     each_target(one_back, drive, "start")
+    for c_ in stores:
+        c_.start()
     each_source(three_back, drive)
     three = diffuse_down(rx3, 6, 2)
     each_source(two_back, drive)
@@ -534,22 +545,17 @@
     four = diffuse_down(eight, 4, 4)
     correction = (part[...] + four[0]) - prev[...]
 
-    stores = []
     for field in range(4):
-        target = c if field == 0 else u.at[field - 1]
-
         m = jnp.where(lax.rem(lane, 4) == field, correction, 0.0)
         m = m + roll(m, 1 if field % 2 == 0 else LANE - 1, 2)
         m = m + roll(m, 2 if field < 2 else LANE - 2, 2)
-        m = jnp.broadcast_to(m[:, None], (4, 4, SUB, LANE)).reshape(NZ, SUB, LANE)
-        for i in range(ROWS):
-            target[H + i, pl.ds(1, NZ)] = target[H + i, pl.ds(1, NZ)] + m
-        for k in range(SUB):
-            cols = pl.ds(LANE * k, LANE)
-            home = ofrac_ref.at[0, :, :, cols] if field == 0 else ovel_ref.at[0, field - 1, :, :, cols]
-            stores.append(pltpu.make_async_copy(
-                target.at[pl.ds(H, ROWS), pl.ds(1, NZ), k, :], home, out_sem.at[field, k]))
-            stores[-1].start()
+        wide[field] = jnp.broadcast_to(m[:, None], (4, 4, SUB, LANE)).reshape(NZ, SUB, LANE)
+    for k in range(SUB):
+        cols = pl.ds(LANE * k, LANE)
+        stores.append(pltpu.make_async_copy(wide.at[0, :, k, :], cfrac_ref.at[:, cols], out_sem.at[2, k]))
+        stores.append(pltpu.make_async_copy(wide.at[1:4, :, k, :], cvel_ref.at[:, :, cols], out_sem.at[3, k]))
+        stores[-2].start()
+        stores[-1].start(priority=1)
     each_target(three_back, drive, "sent")
     each_target(two_back, drive, "sent")
     each_target(one_back, drive, "sent")
@@ -559,6 +565,11 @@
         c_.wait()
 
 
+def add_kernel(frac_ref, vel_ref, frac_off, vel_off, ofrac_ref, ovel_ref):
+    ofrac_ref[...] = frac_ref[...] + frac_off[...][None, None]
+    ovel_ref[...] = vel_ref[...] + vel_off[...][None, :, None]
+
+
 def shards(fraction_levels, start_velocity, electrode_plan):
     line = (SUB, LANE)
     pad = (EXT, NZ + 2) + line
@@ -568,18 +579,20 @@
     def vmem(*shape):
         return pltpu.VMEM(shape, F32)
 
-    return pl.pallas_call(
+    end_fraction, end_velocity, fraction_off, velocity_off = pl.pallas_call(
         kernel,
         out_shape=(
             jax.ShapeDtypeStruct(fraction_levels.shape, F32),
             jax.ShapeDtypeStruct(start_velocity.shape, F32),
+            jax.ShapeDtypeStruct(fraction_levels.shape[2:], F32),
+            jax.ShapeDtypeStruct((3,) + fraction_levels.shape[2:], F32),
         ),
         in_specs=[
             pl.BlockSpec(memory_space=pl.ANY),
             pl.BlockSpec(memory_space=pl.ANY),
             pl.BlockSpec(memory_space=pltpu.SMEM),
         ],
-        out_specs=(pl.BlockSpec(memory_space=pl.ANY), pl.BlockSpec(memory_space=pl.ANY)),
+        out_specs=(pl.BlockSpec(memory_space=pl.ANY),) * 4,
         scratch_shapes=[
             pltpu.VMEM((ROWS, NZ) + line, jnp.int32),
             vmem(*pad), vmem(*pad),
@@ -589,8 +602,8 @@
             vmem(FINE, 3, *line), vmem(NZ, *line),
             vmem(5, *row), vmem(*row), vmem(*row),
             vmem(5, *row), vmem(9, *row), vmem(13, *row), vmem(9, *row), vmem(17, *row),
-            vmem(*row), vmem(17, *row), vmem(17, *row),
-            pltpu.SemaphoreType.DMA((4, SUB)), pltpu.SemaphoreType.DMA((4, SUB)),
+            vmem(*row), vmem(17, *row), vmem(17, *row), vmem(4, NZ, *line),
+            pltpu.SemaphoreType.DMA((2, ROWS, SUB)), pltpu.SemaphoreType.DMA((4, SUB)),
             pltpu.SemaphoreType.DMA((30, 2)), pltpu.SemaphoreType.DMA((30, 2)),
             pltpu.SemaphoreType.DMA((58,)), pltpu.SemaphoreType.DMA((58,)),
             pltpu.SemaphoreType.REGULAR((4,)),
@@ -599,6 +612,29 @@
             collective_id=0, has_side_effects=True, vmem_limit_bytes=62 * 2**20
         ),
     )(fraction_levels, start_velocity, electrode_plan)
+    def frac(i):
+        return 0, i, 0, 0
+
+    def vel(i):
+        return 0, 0, i, 0, 0
+
+    layers, columns = fraction_levels.shape[2:]
+    frac_spec = pl.BlockSpec((1, 2, layers, columns), frac)
+    vel_spec = pl.BlockSpec((1, 3, 2, layers, columns), vel)
+    return pl.pallas_call(
+        add_kernel,
+        grid=(ROWS // 2,),
+        out_shape=(
+            jax.ShapeDtypeStruct(end_fraction.shape, F32),
+            jax.ShapeDtypeStruct(end_velocity.shape, F32),
+        ),
+        in_specs=[
+            frac_spec, vel_spec,
+            pl.BlockSpec((layers, columns), lambda i: (0, 0)),
+            pl.BlockSpec((3, layers, columns), lambda i: (0, 0, 0)),
+        ],
+        out_specs=(frac_spec, vel_spec),
+    )(end_fraction, end_velocity, fraction_off, velocity_off)
 
 
 def solution(mesh):

time: 72.7 us -> 71.2 us (0.979)
  local copies, waits for them, and re-layouts: 3.76 us -> 0 us
  Pallas kernels: 68 us -> 70.3 us
    unnamed x2 -> x0, local copies, waits for them, and re-layouts: 3.76 us -> none
    pallas_call x0 -> x1, Pallas kernels: none -> 2.17 us  [shards(): pl.pallas_call(add_kernel, grid=(ROWS // 2,), out_shape=(jax.ShapeDtypeSt...]
where the time goes in v5:
time: 71.2 us; the launch traced here: 71 us
  Pallas kernels  70.3 us (99%)
    pallas_call x1, Pallas kernels, shards(): pl.pallas_call(kernel, out_shape=(jax.ShapeDtypeStruct(fraction_levels.sh...  68.1 us
    pallas_call x1, Pallas kernels, shards(): pl.pallas_call(add_kernel, grid=(ROWS // 2,), out_shape=(jax.ShapeDtypeSt...  2.17 us

profile of v5, /device:TPU:126, one launch (start us, length us, event | category | flops | bytes accessed | tf_op | source)
XLA Modules:
  0.0 71.0 jit_solution(10130672690284262481)
XLA Ops:
  0.6 68.1 %shard_map.50 = (f32[1,4,16,1024]{3,2,1,0:T(8,128)}, f32[1,3,4,16,1024]{4,3,2,1,0:T(8,128)}, f32[16,1024]{1,0:T(8,128)}, f32[3,16,1024]{2,1,0:T(8,128)}) custom-call(s32[1,4,16,1024]{3,2,1,0:T(8,128)} %lev_ref.1, f32[1,3,4,16,1024]{4,3,2,1,0:T(8,128)} %vel_ref.1, s32[2,4,32]{2,1,0:T(4,128)} %plan_ref.1), custom_call_target="tpu_custom_call" | custom-call | tf_op jit(solution)/shard_map/pallas_call | solution.py:582
  68.8 2.2 %shard_map.51 = (f32[1,4,16,1024]{3,2,1,0:T(8,128)}, f32[1,3,4,16,1024]{4,3,2,1,0:T(8,128)}) custom-call(f32[1,4,16,1024]{3,2,1,0:T(8,128)} %get-tuple-element.6.frac_ref, f32[1,3,4,16,1024]{4,3,2,1,0:T(8,128)} %get-tuple-element.7.vel_ref, f32[16,1024]{1,0:T(8,128)} %get-tuple-element.8.frac_off, f32[3,16,1024]{2,1,0:T(8,128)} %get-tuple-element.9.vel_off), custom_call_target="tpu_custom_call" | custom-call | tf_op jit(solution)/shard_map/pallas_call | solution.py:624

commit v6 on v5

--- a/solution.py
+++ b/solution.py
@@ -20,7 +20,6 @@
 STRIPS = 32
 FINE = 2
 U = 16
-BLOCKS = NZ // U
 
 SLICES, SPACE = 8, 32
 wall_scale = 1.5 * 0.25 * 0.5
@@ -237,7 +236,17 @@
     def each_target(link, src, action):
         dst, reach, dt, base, lo, hi = link
 
-        @pl.when((t >= lo) & (t <= hi))
+        mine = (t >= lo) & (t <= hi)
+        all_there = mine & (s >= reach) & (s < SPACE - reach)
+
+        @pl.when(all_there)
+        def _():
+            for ds in range(-reach, reach + 1):
+                if dt != 0 or ds != 0:
+                    c = coarse_copy(link, src, ds)
+                    c.start() if action == "start" else c.wait_send()
+
+        @pl.when(mine & jnp.logical_not(all_there))
         def _():
             def one(j, _):
                 ds = j - reach
@@ -256,7 +265,16 @@
     def each_source(link, src):
         dst, reach, dt, base, lo, hi = link
 
-        @pl.when((t - dt >= lo) & (t - dt <= hi))
+        mine = (t - dt >= lo) & (t - dt <= hi)
+        all_there = mine & (s >= reach) & (s < SPACE - reach)
+
+        @pl.when(all_there)
+        def _():
+            for ds in range(-reach, reach + 1):
+                if dt != 0 or ds != 0:
+                    coarse_copy(link, src, ds).wait_recv()
+
+        @pl.when(mine & jnp.logical_not(all_there))
         def _():
             def one(j, _):
                 ds = reach - j
@@ -284,10 +302,11 @@
     def over(rows, body):
         lo, hi = rows
 
-        def one(j, _):
-            body(lo + lax.div(j, BLOCKS), U * lax.rem(j, BLOCKS))
+        def pair(j, _):
+            body(lo + 2 * j, 0)
+            body(lo + 2 * j + 1, 0)
             return 0
-        lax.fori_loop(0, (hi - lo) * BLOCKS, one, 0)
+        lax.fori_loop(0, (hi - lo) // 2, pair, 0)
 
     def six(ref, e, z0):
         mid = ref[e, pl.ds(z0, U + 2)]
@@ -499,11 +518,16 @@
         both(sweep_3, H - 1, last + 1)
         sent(near)
         sent(far)
-        over((H, H + ROWS), lambda e, z0: project(new_c, e, z0))
+        def end(e, z0):
+            project(new_c, e, z0)
+
+        both(end, H, last)
         if f == 0:
             near = row_copies([(u.at[0], 0, 1), (u.at[1], 0, 1), (u.at[2], 0, 1)], 26)
+            start(near)
+        over((H + 1, last), end)
+        if f == 0:
             far = row_copies([(u.at[0], 1, 1)], 29)
-            start(near)
             start(far)
         for copies in (fraction_mid, fraction_far, pressure_mid, pressure_near, pressure_far):
             sent(copies)

time: 71.2 us -> 69.9 us (0.982)
  Pallas kernels: 70.3 us -> 69 us
    pallas_call x1, Pallas kernels: 68.1 us -> 66.9 us  [shards(): pl.pallas_call(kernel, out_shape=(jax.ShapeDtypeStruct(fraction_levels.sh...]
where the time goes in v6:
time: 69.9 us; the launch traced here: 69.7 us
  Pallas kernels  69 us (99%)
    pallas_call x1, Pallas kernels, shards(): pl.pallas_call(kernel, out_shape=(jax.ShapeDtypeStruct(fraction_levels.sh...  66.9 us
    pallas_call x1, Pallas kernels, shards(): pl.pallas_call(add_kernel, grid=(ROWS // 2,), out_shape=(jax.ShapeDtypeSt...  2.17 us

profile of v6, /device:TPU:126, one launch (start us, length us, event | category | flops | bytes accessed | tf_op | source)
XLA Modules:
  0.0 69.7 jit_solution(8017988646105663891)
XLA Ops:
  0.6 66.9 %shard_map.50 = (f32[1,4,16,1024]{3,2,1,0:T(8,128)}, f32[1,3,4,16,1024]{4,3,2,1,0:T(8,128)}, f32[16,1024]{1,0:T(8,128)}, f32[3,16,1024]{2,1,0:T(8,128)}) custom-call(s32[1,4,16,1024]{3,2,1,0:T(8,128)} %lev_ref.1, f32[1,3,4,16,1024]{4,3,2,1,0:T(8,128)} %vel_ref.1, s32[2,4,32]{2,1,0:T(4,128)} %plan_ref.1), custom_call_target="tpu_custom_call" | custom-call | tf_op jit(solution)/shard_map/pallas_call | solution.py:606
  67.5 2.2 %shard_map.51 = (f32[1,4,16,1024]{3,2,1,0:T(8,128)}, f32[1,3,4,16,1024]{4,3,2,1,0:T(8,128)}) custom-call(f32[1,4,16,1024]{3,2,1,0:T(8,128)} %get-tuple-element.6.frac_ref, f32[1,3,4,16,1024]{4,3,2,1,0:T(8,128)} %get-tuple-element.7.vel_ref, f32[16,1024]{1,0:T(8,128)} %get-tuple-element.8.frac_off, f32[3,16,1024]{2,1,0:T(8,128)} %get-tuple-element.9.vel_off), custom_call_target="tpu_custom_call" | custom-call | tf_op jit(solution)/shard_map/pallas_call | solution.py:648

commit v7 on v6

--- a/solution.py
+++ b/solution.py
@@ -643,11 +643,11 @@
         return 0, 0, i, 0, 0
 
     layers, columns = fraction_levels.shape[2:]
-    frac_spec = pl.BlockSpec((1, 2, layers, columns), frac)
-    vel_spec = pl.BlockSpec((1, 3, 2, layers, columns), vel)
+    frac_spec = pl.BlockSpec((1, ROWS, layers, columns), frac)
+    vel_spec = pl.BlockSpec((1, 3, ROWS, layers, columns), vel)
     return pl.pallas_call(
         add_kernel,
-        grid=(ROWS // 2,),
+        grid=(1,),
         out_shape=(
             jax.ShapeDtypeStruct(end_fraction.shape, F32),
             jax.ShapeDtypeStruct(end_velocity.shape, F32),

time: 69.9 us -> 70 us (level)
  no operation moved by 1% of the time
where the time goes in v7:
time: 70 us; the launch traced here: 69.8 us
  Pallas kernels  69.1 us (99%)
    pallas_call x1, Pallas kernels, shards(): pl.pallas_call(kernel, out_shape=(jax.ShapeDtypeStruct(fraction_levels.sh...  66.9 us
    pallas_call x1, Pallas kernels, shards(): pl.pallas_call(add_kernel, grid=(1,), out_shape=(jax.ShapeDtypeStruct(end...  2.25 us

profile of v7, /device:TPU:126, one launch (start us, length us, event | category | flops | bytes accessed | tf_op | source)
XLA Modules:
  0.0 69.8 jit_solution(6049526006166205618)
XLA Ops:
  0.6 66.9 %shard_map.50 = (f32[1,4,16,1024]{3,2,1,0:T(8,128)}, f32[1,3,4,16,1024]{4,3,2,1,0:T(8,128)}, f32[16,1024]{1,0:T(8,128)}, f32[3,16,1024]{2,1,0:T(8,128)}) custom-call(s32[1,4,16,1024]{3,2,1,0:T(8,128)} %lev_ref.1, f32[1,3,4,16,1024]{4,3,2,1,0:T(8,128)} %vel_ref.1, s32[2,4,32]{2,1,0:T(4,128)} %plan_ref.1), custom_call_target="tpu_custom_call" | custom-call | tf_op jit(solution)/shard_map/pallas_call | solution.py:606
  67.5 2.3 %shard_map.51 = (f32[1,4,16,1024]{3,2,1,0:T(8,128)}, f32[1,3,4,16,1024]{4,3,2,1,0:T(8,128)}) custom-call(f32[1,4,16,1024]{3,2,1,0:T(8,128)} %get-tuple-element.6.frac_ref, f32[1,3,4,16,1024]{4,3,2,1,0:T(8,128)} %get-tuple-element.7.vel_ref, f32[16,1024]{1,0:T(8,128)} %get-tuple-element.8.frac_off, f32[3,16,1024]{2,1,0:T(8,128)} %get-tuple-element.9.vel_off), custom_call_target="tpu_custom_call" | custom-call | tf_op jit(solution)/shard_map/pallas_call | solution.py:648
